TPU v7x, 128 devices: a whole 4x4x4 slice. The times are simulated.
128 devices in a mesh: dp: 4 (over z), mem: 32 (over x, y, core).
Axes of the slice: x: 4, y: 4, z: 4, core: 2. Of those that a mesh axis runs over, the one named last changes fastest.
Arguments:
- queries: bfloat16 [8192, 2048], P('dp'), may hold values from -9 to 9
- grad_out: bfloat16 [8192, 2048], P('dp'), may hold values from -192 to 192
- mem_keys: bfloat16 [16384, 2048], P('mem'), may hold values from -4 to 4
- mem_values: bfloat16 [16384, 2048], P('mem'), may hold values from -6 to 6
- block_lists: int32 [64, 16], P('dp'), may hold values from 0 to 127, all different within a row
- block_home: int32 [128], replicated, may hold values from 0 to 127, each once
Outputs:
- grad_queries: bfloat16 [8192, 2048], P(('dp', 'mem'))
- grad_keys: bfloat16 [16384, 2048], P('mem')
- grad_values: bfloat16 [16384, 2048], P('mem')
Inputs may be any that keep to these rules, and one draw needn't show every extreme that they name: `block_lists`: each row names 16 different memory blocks; every block is named by some row, some blocks far more often than others. `block_home`: each stored block holds exactly one memory block; stored block j lies on index j // 4 of mem.
All inputs are finite; a program needn't handle non-finite values.
Results may differ from a plain program's by a relative error of at most 0.0085.
Values may be sent and summed in bfloat16 or wider, within the bound.
No kernel may reach another device: no remote copies, remote signals or barrier semaphores. Data moves between devices by JAX's collectives and lax.ppermute only.
A program may use at most 192 MiB of HBM per device.

v0:
```python
import jax
import jax.numpy as jnp
from jax import lax
from jax.experimental import pallas as pl
from jax.experimental.pallas import tpu as pltpu
from jax.sharding import PartitionSpec as P

H = 16
DH = 128
BLK = 128
TOPB = 16
NZ = 4
NCHIP = 16
QPER = 8
NQ = NZ * QPER
NB = 2 * NCHIP
NENT = NQ * TOPB
UNROLL_F = 8
UNROLL_B = 4
SCALE = DH ** (-0.5)
BF = jnp.bfloat16
F32 = jnp.float32
MB = 1 << 20


NT = (((1,), (1,)), ((), ()))
NN = (((1,), (0,)), ((), ()))
TN = (((0,), (0,)), ((), ()))


def dot(a, b, dims):
    return lax.dot_general(a, b, dims, preferred_element_type=F32)


def over_z(array, shift):
    return lax.ppermute(array, "dp", [(i, (i + shift) % NZ) for i in range(NZ)])


def swap_cores(array):
    return lax.ppermute(array, "mem", [(i, i ^ 1) for i in range(2 * NCHIP)])


def plane_exchange(array):
    groups = [[2 * c + k for c in range(NCHIP)] for k in range(2)]
    return lax.all_to_all(array, "mem", 0, 0, axis_index_groups=groups)


def list_kernel(place, l0, l1, l2, l3, home, ents, count):
    z = place[0]
    k = place[1]

    def group(r, lists, n):
        def block(i, n):
            q = r * QPER + i
            seen = jnp.int32(0)
            for t in range(TOPB):
                slot = home[lists[i, t]]
                mine = (slot & 3) == z
                owner = slot >> 2
                b = ((owner & 1) ^ k) * NCHIP + (owner >> 1)
                ents[n] = (q << 15) | ((seen * NQ + q) << 5) | b
                step = mine.astype(jnp.int32)
                n = n + step
                seen = seen + step
            return n

        return lax.fori_loop(0, QPER, block, n)

    n = jnp.int32(0)
    for r, lists in enumerate((l0, l1, l2, l3)):
        n = group(r, lists, n)
    for u in range(8):
        ents[n + u] = (NQ << 15) | (NENT << 5)
    count[0] = n


def make_list(place, lists, home):
    smem = pl.BlockSpec(memory_space=pltpu.SMEM)
    return pl.pallas_call(
        list_kernel,
        out_shape=(
            jax.ShapeDtypeStruct((NENT + 8,), jnp.int32),
            jax.ShapeDtypeStruct((8,), jnp.int32),
        ),
        in_specs=[smem] * 6,
        out_specs=(smem, smem),
        name="entry_list",
    )(place, *lists, home)


def fetch(qrefs, grefs, kvrefs, qs, gs, kv, sems):
    copies = []
    for r in range(NZ):
        copies.append(pltpu.make_async_copy(qrefs[r], qs.at[r], sems.at[r]))
        copies.append(pltpu.make_async_copy(grefs[r], gs.at[r], sems.at[NZ + r]))
    for p in range(4):
        to = kv.at[p % 2, p // 2]
        copies.append(pltpu.make_async_copy(kvrefs[p], to, sems.at[2 * NZ + p]))
    for copy in copies:
        copy.start()
    return copies


def unpack(p):
    q = p >> 15
    b = p & 31
    return (q >> 3) & 3, q & 7, q, (p >> 5) & 1023, b >> 4, b & 15


def fwd_kernel(ents, count, q0, q1, q2, q3, g0, g1, g2, g3, ka, va, kb, vb, out, qs, gs, kv, st, sems):
    copies = fetch((q0, q1, q2, q3), (g0, g1, g2, g3), (ka, va, kb, vb), qs, gs, kv, sems)
    st[0] = jnp.full((NENT + 8, DH), -1e30, F32)
    st[1] = jnp.zeros((NENT + 8, DH), F32)
    st[2] = jnp.zeros((NENT + 8, DH), F32)
    for copy in copies:
        copy.wait()

    def body(n, carry):
        parts = [unpack(ents[UNROLL_F * n + u]) for u in range(UNROLL_F)]
        scores = [dot(kv[0, p[4], p[5]], qs[p[0], p[1]], NT) * SCALE for p in parts]
        dprob = [dot(kv[1, p[4], p[5]], gs[p[0], p[1]], NT) for p in parts]
        highs = [jnp.max(x, axis=0, keepdims=True) for x in scores]
        expo = [jnp.exp(x - high) for x, high in zip(scores, highs)]
        for p, high, e, d in zip(parts, highs, expo, dprob):
            row = pl.ds(p[3], 1)
            st[0, row, :] = high
            st[1, row, :] = jnp.sum(e, axis=0, keepdims=True)
            st[2, row, :] = jnp.sum(e.astype(BF).astype(F32) * d, axis=0, keepdims=True)
        return carry

    lax.fori_loop(0, (count[0] + UNROLL_F - 1) // UNROLL_F, body, 0)
    high = st[0, 0:NQ]
    for e in range(1, TOPB):
        high = jnp.maximum(high, st[0, e * NQ : (e + 1) * NQ])
    total = jnp.zeros((NQ, DH), F32)
    prod = jnp.zeros((NQ, DH), F32)
    for e in range(TOPB):
        rows = slice(e * NQ, (e + 1) * NQ)
        weight = jnp.exp(st[0, rows] - high)
        total = total + weight * st[1, rows]
        prod = prod + weight * st[2, rows]
    out[0] = high
    out[1] = total
    out[2] = prod


def scratch_in():
    return [
        pltpu.VMEM((NZ, QPER, BLK, DH), BF),
        pltpu.VMEM((NZ, QPER, BLK, DH), BF),
        pltpu.VMEM((2, 2, NCHIP, BLK, DH), BF),
    ]


def forward(ents, count, qparts, gparts, kvs):
    smem = pl.BlockSpec(memory_space=pltpu.SMEM)
    far = pl.BlockSpec(memory_space=pl.ANY)
    return pl.pallas_call(
        fwd_kernel,
        out_shape=jax.ShapeDtypeStruct((3, NQ, DH), F32),
        in_specs=[smem, smem] + [far] * 12,
        out_specs=pl.BlockSpec(memory_space=pltpu.VMEM),
        scratch_shapes=scratch_in()
        + [pltpu.VMEM((3, NENT + 8, DH), F32), pltpu.SemaphoreType.DMA((2 * NZ + 4,))],
        compiler_params=pltpu.CompilerParams(vmem_limit_bytes=24 * MB),
        name="forward",
    )(ents, count, *qparts, *gparts, *kvs)


def bwd_kernel(
    ents, count, s0, s1, s2, s3, q0, q1, q2, q3, g0, g1, g2, g3, ka, va, kb, vb,
    dq0, dq1, dq2, dq3, kown, vown, kother, vother,
    qs, gs, kv, dq, dk, dv, lse, delta, sems,
):
    copies = fetch((q0, q1, q2, q3), (g0, g1, g2, g3), (ka, va, kb, vb), qs, gs, kv, sems)

    def clear(i, carry):
        zero = jnp.zeros((BLK, DH), F32)
        dq[i] = zero
        dk[i] = zero
        dv[i] = zero
        return carry

    lax.fori_loop(0, NQ, clear, 0)
    for r in range(NZ):
        rows = slice(r * QPER, (r + 1) * QPER)
        parts = []
        for ref, shift in ((s0, 0), (s1, 1), (s2, 2), (s3, 3)):
            at = (r + shift) % NZ
            parts.append([ref[n, at * QPER : (at + 1) * QPER] for n in range(3)])
        high = jnp.maximum(
            jnp.maximum(parts[0][0], parts[1][0]), jnp.maximum(parts[2][0], parts[3][0])
        )
        total = jnp.zeros((QPER, DH), F32)
        prod = jnp.zeros((QPER, DH), F32)
        for part in parts:
            weight = jnp.exp(part[0] - high)
            total = total + weight * part[1]
            prod = prod + weight * part[2]
        lse[rows] = high + jnp.log(total)
        delta[rows] = prod / total
    for copy in copies:
        copy.wait()

    lse[NQ : NQ + 8] = jnp.full((8, DH), 1e30, F32)
    delta[NQ : NQ + 8] = jnp.zeros((8, DH), F32)

    def body(n, carry):
        parts = [unpack(ents[UNROLL_B * n + u]) for u in range(UNROLL_B)]
        keys = [kv[0, p[4], p[5]] for p in parts]
        quer = [qs[p[0], p[1]] for p in parts]
        grad = [gs[p[0], p[1]] for p in parts]
        scores = [dot(a, b, NT) * SCALE for a, b in zip(keys, quer)]
        dprob = [dot(kv[1, p[4], p[5]], b, NT) for p, b in zip(parts, grad)]
        probs = [jnp.exp(x - lse[pl.ds(p[2], 1), :]) for x, p in zip(scores, parts)]
        dscore = [
            (x * (d - delta[pl.ds(p[2], 1), :]) * SCALE).astype(BF)
            for x, d, p in zip(probs, dprob, parts)
        ]
        gv = [dot(x.astype(BF), b, NN) for x, b in zip(probs, grad)]
        gk = [dot(x, b, NN) for x, b in zip(dscore, quer)]
        gq = [dot(x, b, TN) for x, b in zip(dscore, keys)]
        for p, a, b, c in zip(parts, gv, gk, gq):
            at = p[4] * NCHIP + p[5]
            dv[at] += a
            dk[at] += b
            dq[p[0] * QPER + p[1]] += c
        return carry

    lax.fori_loop(0, (count[0] + UNROLL_B - 1) // UNROLL_B, body, 0)
    for r, ref in enumerate((dq0, dq1, dq2, dq3)):
        ref[...] = dq[r * QPER : (r + 1) * QPER].astype(ref.dtype)
    kown[...] = dk[:NCHIP]
    vown[...] = dv[:NCHIP]
    kother[...] = dk[NCHIP:].astype(BF)
    vother[...] = dv[NCHIP:].astype(BF)


def backward(ents, count, stats, qparts, gparts, kvs):
    smem = pl.BlockSpec(memory_space=pltpu.SMEM)
    vmem = pl.BlockSpec(memory_space=pltpu.VMEM)
    far = pl.BlockSpec(memory_space=pl.ANY)
    tile = (BLK, DH)
    outs = [jax.ShapeDtypeStruct((QPER,) + tile, F32)]
    outs += [jax.ShapeDtypeStruct((QPER,) + tile, BF)] * 3
    outs += [jax.ShapeDtypeStruct((NCHIP,) + tile, F32)] * 2
    outs += [jax.ShapeDtypeStruct((NCHIP,) + tile, BF)] * 2
    return pl.pallas_call(
        bwd_kernel,
        out_shape=tuple(outs),
        in_specs=[smem, smem] + [vmem] * 4 + [far] * 12,
        out_specs=tuple([vmem] * 8),
        scratch_shapes=scratch_in()
        + [
            pltpu.VMEM((NQ,) + tile, F32),
            pltpu.VMEM((NB,) + tile, F32),
            pltpu.VMEM((NB,) + tile, F32),
            pltpu.VMEM((NQ + 8, DH), F32),
            pltpu.VMEM((NQ + 8, DH), F32),
            pltpu.SemaphoreType.DMA((2 * NZ + 4,)),
        ],
        compiler_params=pltpu.CompilerParams(vmem_limit_bytes=40 * MB),
        name="backward",
    )(ents, count, *stats, *qparts, *gparts, *kvs)


def place_kernel(place, k0, k1, k2, k3, v0, v1, v2, v3, outk, outv, sems):
    z = place[0]
    copies = []
    for r, (kr, vr) in enumerate(((k0, v0), (k1, v1), (k2, v2), (k3, v3))):
        rows = pl.ds(pl.multiple_of(((z + r) & 3) * BLK, BLK), BLK)
        copies.append(pltpu.make_async_copy(kr, outk.at[rows], sems.at[2 * r]))
        copies.append(pltpu.make_async_copy(vr, outv.at[rows], sems.at[2 * r + 1]))
    for copy in copies:
        copy.start()
    for copy in copies:
        copy.wait()


def place_blocks(place, kparts, vparts):
    smem = pl.BlockSpec(memory_space=pltpu.SMEM)
    far = pl.BlockSpec(memory_space=pl.ANY)
    shape = jax.ShapeDtypeStruct((NZ * BLK, H * DH), BF)
    return pl.pallas_call(
        place_kernel,
        out_shape=(shape, shape),
        in_specs=[smem] + [pl.BlockSpec(memory_space=pltpu.VMEM)] * 8,
        out_specs=(far, far),
        scratch_shapes=[pltpu.SemaphoreType.DMA((2 * NZ,))],
        compiler_params=pltpu.CompilerParams(vmem_limit_bytes=16 * MB),
        name="place_blocks",
    )(place, *kparts, *vparts)


def heads_first(array):
    return jnp.transpose(array.reshape(array.shape[0], H, DH), (1, 0, 2))


def rows_first(array):
    return jnp.transpose(array, (1, 0, 2)).reshape(array.shape[1], H * DH)


def per_device(queries, grad_out, mem_keys, mem_values, block_lists, block_home):
    z = lax.axis_index("dp")
    m = lax.axis_index("mem")
    c, k = m // 2, m % 2
    place = jnp.stack([z, k]).astype(jnp.int32)

    kz = heads_first(lax.dynamic_slice_in_dim(mem_keys, z * BLK, BLK, 0))
    vz = heads_first(lax.dynamic_slice_in_dim(mem_values, z * BLK, BLK, 0))
    k_got, v_got = plane_exchange(kz), plane_exchange(vz)

    rows = QPER * BLK
    mine = (k * rows, c * DH)
    tiles = (QPER, BLK, DH)
    q_own = lax.dynamic_slice(queries, mine, (rows, DH)).reshape(tiles)
    g_own = lax.dynamic_slice(grad_out, mine, (rows, DH)).reshape(tiles)
    l_own = lax.dynamic_slice_in_dim(block_lists, k * QPER, QPER, 0)
    q_prev = over_z(q_own, 1)
    g_next = over_z(g_own, -1)
    g_prev = over_z(g_own, 1)
    q_next = over_z(q_own, -1)
    q_far = over_z(q_prev, 1)
    g_far = over_z(g_next, -1)
    lists = (l_own, over_z(l_own, -1), over_z(l_own, 2), over_z(l_own, 1))
    ents, count = make_list(place, lists, block_home)
    qparts = (q_own, q_next, q_far, q_prev)
    gparts = (g_own, g_next, g_far, g_prev)
    kvs = (k_got, v_got, swap_cores(k_got), swap_cores(v_got))

    stat = forward(ents, count, qparts, gparts, kvs)
    stats = (stat, over_z(stat, 1), over_z(stat, 2), over_z(stat, -1))
    dq0, dq1, dq2, dq3, kown, vown, kother, vother = backward(
        ents, count, stats, qparts, gparts, kvs
    )

    v_sum = (vown + swap_cores(vother).astype(F32)).astype(BF)
    k_sum = (kown + swap_cores(kother).astype(F32)).astype(BF)
    v_own = rows_first(plane_exchange(v_sum))
    k_own = rows_first(plane_exchange(k_sum))
    v_prev = over_z(v_own, 1)
    v_next = over_z(v_own, -1)
    k_prev = over_z(k_own, 1)
    k_next = over_z(k_own, -1)
    v_far = over_z(v_prev, 1)
    k_far = over_z(k_next, -1)
    grad_keys, grad_values = place_blocks(
        place, (k_own, k_next, k_far, k_prev), (v_own, v_next, v_far, v_prev)
    )

    dq_sum = (
        dq0
        + over_z(dq1, 1).astype(F32)
        + over_z(dq3, -1).astype(F32)
        + over_z(dq2, 2).astype(F32)
    ).astype(BF)
    half = BLK // 2
    keep = lax.dynamic_slice_in_dim(dq_sum, k * half, half, 1)
    give = lax.dynamic_slice_in_dim(dq_sum, (1 - k) * half, half, 1)
    got = swap_cores(give)
    whole = jnp.where(
        k == 0, jnp.concatenate([keep, got], axis=0), jnp.concatenate([got, keep], axis=0)
    )
    grad_queries = rows_first(plane_exchange(whole))
    return grad_queries, grad_keys, grad_values


def solution(mesh):
    in_specs = (P("dp", None), P("dp", None), P("mem", None), P("mem", None), P("dp", None), P())
    out_specs = (P(("dp", "mem"), None), P("mem", None), P("mem", None))
    return jax.shard_map(
        per_device, mesh=mesh, in_specs=in_specs, out_specs=out_specs, check_vma=False
    )
```

profile of v0, /device:TPU:0, one launch (start us, length us, event | category | flops | bytes accessed | tf_op | source)
XLA Modules:
  0.0 175.4 jit_solution(2379169963157219700)
XLA Ops:
  3.2 7.1 %all-to-all-start = ((bf16[16,128,128]{2,1,0:T(8,128)(2,1)}), bf16[16,128,128]{2,1,0:T(8,128)(2,1)S(1)}, u32[]{:S(2)}, u32[]{:S(2)}) async-start(bf16[16,128,128]{2,1,0:T(8,128)(2,1)} %bitcast.5), calls=%async_computation | async-start | bytes 1048576 | tf_op jit(solution)/shard_map/all_to_all | solution.py:45
  11.7 10.2 %all-to-all-done.ka = bf16[16,128,128]{2,1,0:T(8,128)(2,1)S(1)} async-done(((bf16[16,128,128]{2,1,0:T(8,128)(2,1)}), bf16[16,128,128]{2,1,0:T(8,128)(2,1)S(1)}, u32[]{:S(2)}, u32[]{:S(2)}) %all-to-all-start) | async-done | bytes 524320 | tf_op jit(solution)/shard_map/all_to_all | solution.py:45
  21.9 3.6 %all-to-all-start.1 = ((bf16[16,128,128]{2,1,0:T(8,128)(2,1)}), bf16[16,128,128]{2,1,0:T(8,128)(2,1)S(1)}, u32[]{:S(2)}, u32[]{:S(2)}) async-start(bf16[16,128,128]{2,1,0:T(8,128)(2,1)} %bitcast.7), calls=%async_computation.1 | async-start | bytes 1048576 | tf_op jit(solution)/shard_map/all_to_all | solution.py:45
  25.5 4.1 %collective-permute-start = (s32[8,16]{1,0:T(8,128)S(1)}, s32[8,16]{1,0:T(8,128)S(1)}, u32[]{:S(2)}, u32[]{:S(2)}) collective-permute-start(s32[8,16]{1,0:T(8,128)S(1)} %constant_dynamic-slice_fusion.4.l0), channel_id=1, source_target_pairs={{0,96},{32,0},{64,32},{96,64},{1,97},{33,1},{65,33},{97,65},{2,98}... | collective-permute-start | bytes 1544 | tf_op jit(solution)/shard_map/ppermute | solution.py:36
  31.8 2.0 %collective-permute-start.3 = (bf16[8,128,128]{2,1,0:T(8,128)(2,1)S(1)}, bf16[8,128,128]{2,1,0:T(8,128)(2,1)S(1)}, u32[]{:S(2)}, u32[]{:S(2)}) collective-permute-start(bf16[8,128,128]{2,1,0:T(8,128)(2,1)S(1)} %bitcast.26), channel_id=1, source_target_pairs={{0,96},{32,0},{64,32},{96,64},{1,97},{33,1},{65,33},{97,65},{2,98}... | collective-permute-start | bytes 786440 | tf_op jit(solution)/shard_map/ppermute | solution.py:36
  35.2 3.0 %collective-permute-start.6 = (bf16[8,128,128]{2,1,0:T(8,128)(2,1)S(1)}, bf16[8,128,128]{2,1,0:T(8,128)(2,1)S(1)}, u32[]{:S(2)}, u32[]{:S(2)}) collective-permute-start(bf16[8,128,128]{2,1,0:T(8,128)(2,1)S(1)} %bitcast.30), channel_id=1, source_target_pairs={{0,96},{32,0},{64,32},{96,64},{1,97},{33,1},{65,33},{97,65},{2,98}... | collective-permute-start | bytes 786440 | tf_op jit(solution)/shard_map/ppermute | solution.py:36
  38.8 2.2 %collective-permute-done.3.q1 = bf16[8,128,128]{2,1,0:T(8,128)(2,1)S(1)} collective-permute-done((bf16[8,128,128]{2,1,0:T(8,128)(2,1)S(1)}, bf16[8,128,128]{2,1,0:T(8,128)(2,1)S(1)}, u32[]{:S(2)}, u32[]{:S(2)}) %collective-permute-start.3) | collective-permute-done | bytes 262176 | tf_op jit(solution)/shard_map/ppermute | solution.py:36
  43.7 3.3 %collective-permute-start.7 = (bf16[8,128,128]{2,1,0:T(8,128)(2,1)S(1)}, bf16[8,128,128]{2,1,0:T(8,128)(2,1)}, u32[]{:S(2)}, u32[]{:S(2)}) collective-permute-start(bf16[8,128,128]{2,1,0:T(8,128)(2,1)S(1)} %collective-permute-done.6.g1), channel_id=1, source_target_pairs={{0,96},{32,0},{64,32},{96,64},{1,97},{33,1},{65,33},{97,65},{2,98}... | collective-permute-start | bytes 786440 | tf_op jit(solution)/shard_map/ppermute | solution.py:36
  47.6 4.7 %entry_list.1 = (s32[520]{0:T(1024)}, s32[8]{0:T(128)}) custom-call(s32[2]{0:T(128)} %pad_add_fusion.place, s32[8,16]{1,0:T(8,128)} %copy-done.16, s32[8,16]{1,0:T(8,128)} %copy-done.17, s32[8,16]{1,0:T(8,128)} %copy-done.18, s32[8,16]{1,0:T(8,128)} %copy-done.19, s32[128]{0:T(128)} %home.1), custom_call_target="tpu_custom_call" | custom-call | tf_op jit(solution)/shard_map/entry_list/pallas_call | solution.py:79
  55.3 10.4 %forward.1.s0 = f32[3,32,128]{2,1,0:T(8,128)S(1)} custom-call(s32[520]{0:T(1024)S(1)} %copy-done.5, s32[8]{0:T(128)S(1)} %copy-done.8, bf16[8,128,128]{2,1,0:T(8,128)(2,1)S(1)} %bitcast.28, bf16[8,128,128]{2,1,0:T(8,128)(2,1)S(1)} %collective-permute-done.3.q1, bf16[8,128,128]{2,1,0:T(8,128)(2,1)} %collective-permute-done.5.q2, ...), custom_call_target="tpu_custom_call" | custom-call | tf_op jit(solution)/shard_map/forward/pallas_call | solution.py:158
  65.9 3.7 %collective-permute-start.12 = (f32[3,32,128]{2,1,0:T(8,128)S(1)}, f32[3,32,128]{2,1,0:T(8,128)S(1)}, u32[]{:S(2)}, u32[]{:S(2)}) collective-permute-start(f32[3,32,128]{2,1,0:T(8,128)S(1)} %forward.1.s0), channel_id=1, source_target_pairs={{0,64},{32,96},{64,0},{96,32},{1,65},{33,97},{65,1},{97,33},{2,66}... | collective-permute-start | bytes 147464 | tf_op jit(solution)/shard_map/ppermute | solution.py:36
  73.6 20.5 %backward.1 = (f32[8,128,128]{2,1,0:T(8,128)S(1)}, bf16[8,128,128]{2,1,0:T(8,128)(2,1)S(1)}, bf16[8,128,128]{2,1,0:T(8,128)(2,1)S(1)}, bf16[8,128,128]{2,1,0:T(8...) custom-call(s32[520]{0:T(1024)S(1)} %copy-done.6, ...), custom_call_target="tpu_custom_call" | custom-call | tf_op jit(solution)/shard_map/backward/pallas_call | solution.py:248
  101.0 7.3 %all-to-all-start.3 = ((bf16[16,128,128]{2,1,0:T(8,128)(2,1)}), bf16[16,128,128]{2,1,0:T(8,128)(2,1)S(1)}, u32[]{:S(2)}, u32[]{:S(2)}) async-start(bf16[16,128,128]{2,1,0:T(8,128)(2,1)} %add_convert_fusion.1), calls=%async_computation.3 | async-start | bytes 1048576 | tf_op jit(solution)/shard_map/all_to_all | solution.py:45
  109.4 3.3 %collective-permute-start.15 = (bf16[8,128,128]{2,1,0:T(8,128)(2,1)S(1)}, bf16[8,128,128]{2,1,0:T(8,128)(2,1)}, u32[]{:S(2)}, u32[]{:S(2)}) collective-permute-start(bf16[8,128,128]{2,1,0:T(8,128)(2,1)S(1)} %copy-done.13), channel_id=1, source_target_pairs={{0,96},{32,0},{64,32},{96,64},{1,97},{33,1},{65,33},{97,65},{2,98}... | collective-permute-start | bytes 786440 | tf_op jit(solution)/shard_map/ppermute | solution.py:36
  114.4 5.6 %all-to-all-done.3 = bf16[16,128,128]{2,1,0:T(8,128)(2,1)S(1)} async-done(((bf16[16,128,128]{2,1,0:T(8,128)(2,1)}), bf16[16,128,128]{2,1,0:T(8,128)(2,1)S(1)}, u32[]{:S(2)}, u32[]{:S(2)}) %all-to-all-start.3) | async-done | bytes 524320 | tf_op jit(solution)/shard_map/all_to_all | solution.py:45
  120.0 4.2 %all-to-all-start.4 = ((bf16[16,128,128]{2,1,0:T(8,128)(2,1)}), bf16[16,128,128]{2,1,0:T(8,128)(2,1)}, u32[]{:S(2)}, u32[]{:S(2)}) async-start(bf16[16,128,128]{2,1,0:T(8,128)(2,1)} %add_convert_fusion), calls=%async_computation.4 | async-start | bytes 1048576 | tf_op jit(solution)/shard_map/all_to_all | solution.py:45
  126.5 3.6 %collective-permute-start.19 = (bf16[128,2048]{1,0:T(8,128)(2,1)S(1)}, bf16[128,2048]{1,0:T(8,128)(2,1)S(1)}, u32[]{:S(2)}, u32[]{:S(2)}) collective-permute-start(bf16[128,2048]{1,0:T(8,128)(2,1)S(1)} %copy_bitcast_fusion.1.k0), channel_id=1, source_target_pairs={{0,96},{32,0},{64,32},{96,64},{1,97},{33,1},{65,33},{97,65},{2,98}... | collective-permute-start | bytes 1572872 | tf_op jit(solution)/shard_map/ppermute | solution.py:36
  130.1 4.5 %all-to-all-done.4 = bf16[16,128,128]{2,1,0:T(8,128)(2,1)} async-done(((bf16[16,128,128]{2,1,0:T(8,128)(2,1)}), bf16[16,128,128]{2,1,0:T(8,128)(2,1)}, u32[]{:S(2)}, u32[]{:S(2)}) %all-to-all-start.4) | async-done | bytes 524320 | tf_op jit(solution)/shard_map/all_to_all | solution.py:45
  138.0 3.5 %all-to-all-start.2 = ((bf16[16,64,128]{2,1,0:T(8,128)(2,1)}), bf16[16,64,128]{2,1,0:T(8,128)(2,1)S(1)}, u32[]{:S(2)}, u32[]{:S(2)}) async-start(bf16[16,64,128]{2,1,0:T(8,128)(2,1)} %maximum_select_fusion), calls=%async_computation.2 | async-start | bytes 524288 | tf_op jit(solution)/shard_map/all_to_all | solution.py:45
  142.6 3.3 %collective-permute-start.23 = (bf16[128,2048]{1,0:T(8,128)(2,1)S(1)}, bf16[128,2048]{1,0:T(8,128)(2,1)S(1)}, u32[]{:S(2)}, u32[]{:S(2)}) collective-permute-start(bf16[128,2048]{1,0:T(8,128)(2,1)S(1)} %copy_bitcast_fusion.v0), channel_id=1, source_target_pairs={{0,96},{32,0},{64,32},{96,64},{1,97},{33,1},{65,33},{97,65},{2,98}... | collective-permute-start | bytes 1572872 | tf_op jit(solution)/shard_map/ppermute | solution.py:36
  147.9 3.9 %collective-permute-done.24.v3 = bf16[128,2048]{1,0:T(8,128)(2,1)S(1)} collective-permute-done((bf16[128,2048]{1,0:T(8,128)(2,1)S(1)}, bf16[128,2048]{1,0:T(8,128)(2,1)S(1)}, u32[]{:S(2)}, u32[]{:S(2)}) %collective-permute-start.24) | collective-permute-done | bytes 524320 | tf_op jit(solution)/shard_map/ppermute | solution.py:36
  152.6 10.5 %collective-permute-done.21.k3 = bf16[128,2048]{1,0:T(8,128)(2,1)S(1)} collective-permute-done((bf16[128,2048]{1,0:T(8,128)(2,1)S(1)}, bf16[128,2048]{1,0:T(8,128)(2,1)S(1)}, u32[]{:S(2)}, u32[]{:S(2)}) %collective-permute-start.21) | collective-permute-done | bytes 524320 | tf_op jit(solution)/shard_map/ppermute | solution.py:36
  163.1 7.5 %collective-permute-done.20.k2 = bf16[128,2048]{1,0:T(8,128)(2,1)} collective-permute-done((bf16[128,2048]{1,0:T(8,128)(2,1)S(1)}, bf16[128,2048]{1,0:T(8,128)(2,1)}, u32[]{:S(2)}, u32[]{:S(2)}) %collective-permute-start.20) | collective-permute-done | bytes 524320 | tf_op jit(solution)/shard_map/ppermute | solution.py:36
  171.9 3.3 %place_blocks.1 = (bf16[512,2048]{1,0:T(8,128)(2,1)}, bf16[512,2048]{1,0:T(8,128)(2,1)}) custom-call(s32[2]{0:T(128)S(1)} %copy-done.7, bf16[128,2048]{1,0:T(8,128)(2,1)S(1)} %copy_bitcast_fusion.1.k0, bf16[128,2048]{1,0:T(8,128)(2,1)S(1)} %collective-permute-done.19.k1, bf16[128,2048]{1,0:T(8,128)(2,1)} %collective-permute-done.20.k2, ...), custom_call_target="tpu_custom_call" | custom-call | tf_op jit(solution)/shard_map/place_blocks/pallas_call | solution.py:284
  (99 shorter events, 38.9 us)
Async XLA Ops:
  3.2 18.6 %all-to-all-start = ((bf16[16,128,128]{2,1,0:T(8,128)(2,1)}), bf16[16,128,128]{2,1,0:T(8,128)(2,1)S(1)}, u32[]{:S(2)}, u32[]{:S(2)}) async-start(bf16[16,128,128]{2,1,0:T(8,128)(2,1)} %bitcast.5), calls=%async_computation | async-start | bytes 1048576 | tf_op jit(solution)/shard_map/all_to_all | solution.py:45
  21.9 16.4 %all-to-all-start.1 = ((bf16[16,128,128]{2,1,0:T(8,128)(2,1)}), bf16[16,128,128]{2,1,0:T(8,128)(2,1)S(1)}, u32[]{:S(2)}, u32[]{:S(2)}) async-start(bf16[16,128,128]{2,1,0:T(8,128)(2,1)} %bitcast.7), calls=%async_computation.1 | async-start | bytes 1048576 | tf_op jit(solution)/shard_map/all_to_all | solution.py:45
  25.5 9.7 %collective-permute-start = (s32[8,16]{1,0:T(8,128)S(1)}, s32[8,16]{1,0:T(8,128)S(1)}, u32[]{:S(2)}, u32[]{:S(2)}) collective-permute-start(s32[8,16]{1,0:T(8,128)S(1)} %constant_dynamic-slice_fusion.4.l0), channel_id=1, source_target_pairs={{0,96},{32,0},{64,32},{96,64},{1,97},{33,1},{65,33},{97,65},{2,98}... | collective-permute-start | bytes 1544 | tf_op jit(solution)/shard_map/ppermute | solution.py:36
  29.6 8.6 %collective-permute-start.2 = (s32[8,16]{1,0:T(8,128)S(1)}, s32[8,16]{1,0:T(8,128)S(1)}, u32[]{:S(2)}, u32[]{:S(2)}) collective-permute-start(s32[8,16]{1,0:T(8,128)S(1)} %constant_dynamic-slice_fusion.4.l0), channel_id=1, source_target_pairs={{0,32},{32,64},{64,96},{96,0},{1,33},{33,65},{65,97},{97,1},{2,34}... | collective-permute-start | bytes 1544 | tf_op jit(solution)/shard_map/ppermute | solution.py:36
  31.8 9.1 %collective-permute-start.3 = (bf16[8,128,128]{2,1,0:T(8,128)(2,1)S(1)}, bf16[8,128,128]{2,1,0:T(8,128)(2,1)S(1)}, u32[]{:S(2)}, u32[]{:S(2)}) collective-permute-start(bf16[8,128,128]{2,1,0:T(8,128)(2,1)S(1)} %bitcast.26), channel_id=1, source_target_pairs={{0,96},{32,0},{64,32},{96,64},{1,97},{33,1},{65,33},{97,65},{2,98}... | collective-permute-start | bytes 786440 | tf_op jit(solution)/shard_map/ppermute | solution.py:36
  33.9 8.8 %collective-permute-start.4 = (bf16[8,128,128]{2,1,0:T(8,128)(2,1)S(1)}, bf16[8,128,128]{2,1,0:T(8,128)(2,1)S(1)}, u32[]{:S(2)}, u32[]{:S(2)}) collective-permute-start(bf16[8,128,128]{2,1,0:T(8,128)(2,1)S(1)} %bitcast.27), channel_id=1, source_target_pairs={{0,32},{32,64},{64,96},{96,0},{1,33},{33,65},{65,97},{97,1},{2,34}... | collective-permute-start | bytes 786440 | tf_op jit(solution)/shard_map/ppermute | solution.py:36
  38.2 15.8 %collective-permute-start.9 = (bf16[16,128,128]{2,1,0:T(8,128)(2,1)S(1)}, bf16[16,128,128]{2,1,0:T(8,128)(2,1)S(1)}, u32[]{:S(2)}, u32[]{:S(2)}) collective-permute-start(bf16[16,128,128]{2,1,0:T(8,128)(2,1)S(1)} %all-to-all-done.ka), channel_id=1, source_target_pairs={{0,1},{1,0},{2,3},{3,2},{4,5},{5,4},{6,7},{7,6},{8,9},{9,8},{10,11... | collective-permute-start | bytes 1572872 | tf_op jit(solution)/shard_map/ppermute | solution.py:40
  38.2 15.8 %collective-permute-start.10 = (bf16[16,128,128]{2,1,0:T(8,128)(2,1)S(1)}, bf16[16,128,128]{2,1,0:T(8,128)(2,1)S(1)}, u32[]{:S(2)}, u32[]{:S(2)}) collective-permute-start(bf16[16,128,128]{2,1,0:T(8,128)(2,1)S(1)} %all-to-all-done.1.va), channel_id=1, source_target_pairs={{0,1},{1,0},{2,3},{3,2},{4,5},{5,4},{6,7},{7,6},{8,9},{9,8},{10,11... | collective-permute-start | bytes 1572872 | tf_op jit(solution)/shard_map/ppermute | solution.py:40
  40.9 11.4 %collective-permute-start.8 = (bf16[8,128,128]{2,1,0:T(8,128)(2,1)S(1)}, bf16[8,128,128]{2,1,0:T(8,128)(2,1)}, u32[]{:S(2)}, u32[]{:S(2)}) collective-permute-start(bf16[8,128,128]{2,1,0:T(8,128)(2,1)S(1)} %bitcast.31), channel_id=1, source_target_pairs={{0,32},{32,64},{64,96},{96,0},{1,33},{33,65},{65,97},{97,1},{2,34}... | collective-permute-start | bytes 786440 | tf_op jit(solution)/shard_map/ppermute | solution.py:36
  42.7 11.3 %collective-permute-start.5 = (bf16[8,128,128]{2,1,0:T(8,128)(2,1)S(1)}, bf16[8,128,128]{2,1,0:T(8,128)(2,1)}, u32[]{:S(2)}, u32[]{:S(2)}) collective-permute-start(bf16[8,128,128]{2,1,0:T(8,128)(2,1)S(1)} %collective-permute-done.4.q3), channel_id=1, source_target_pairs={{0,32},{32,64},{64,96},{96,0},{1,33},{33,65},{65,97},{97,1},{2,34}... | collective-permute-start | bytes 786440 | tf_op jit(solution)/shard_map/ppermute | solution.py:36
  43.7 10.3 %collective-permute-start.7 = (bf16[8,128,128]{2,1,0:T(8,128)(2,1)S(1)}, bf16[8,128,128]{2,1,0:T(8,128)(2,1)}, u32[]{:S(2)}, u32[]{:S(2)}) collective-permute-start(bf16[8,128,128]{2,1,0:T(8,128)(2,1)S(1)} %collective-permute-done.6.g1), channel_id=1, source_target_pairs={{0,96},{32,0},{64,32},{96,64},{1,97},{33,1},{65,33},{97,65},{2,98}... | collective-permute-start | bytes 786440 | tf_op jit(solution)/shard_map/ppermute | solution.py:36
  98.1 15.3 %collective-permute-start.22 = (bf16[16,128,128]{2,1,0:T(8,128)(2,1)}, bf16[16,128,128]{2,1,0:T(8,128)(2,1)S(1)}, u32[]{:S(2)}, u32[]{:S(2)}) collective-permute-start(bf16[16,128,128]{2,1,0:T(8,128)(2,1)} %get-tuple-element.24), channel_id=1, source_target_pairs={{0,1},{1,0},{2,3},{3,2},{4,5},{5,4},{6,7},{7,6},{8,9},{9,8},{10,11... | collective-permute-start | bytes 1572872 | tf_op jit(solution)/shard_map/ppermute | solution.py:40
  101.0 19.1 %all-to-all-start.3 = ((bf16[16,128,128]{2,1,0:T(8,128)(2,1)}), bf16[16,128,128]{2,1,0:T(8,128)(2,1)S(1)}, u32[]{:S(2)}, u32[]{:S(2)}) async-start(bf16[16,128,128]{2,1,0:T(8,128)(2,1)} %add_convert_fusion.1), calls=%async_computation.3 | async-start | bytes 1048576 | tf_op jit(solution)/shard_map/all_to_all | solution.py:45
  108.3 16.0 %collective-permute-start.16 = (bf16[8,128,128]{2,1,0:T(8,128)(2,1)S(1)}, bf16[8,128,128]{2,1,0:T(8,128)(2,1)}, u32[]{:S(2)}, u32[]{:S(2)}) collective-permute-start(bf16[8,128,128]{2,1,0:T(8,128)(2,1)S(1)} %copy-done.15), channel_id=1, source_target_pairs={{0,64},{32,96},{64,0},{96,32},{1,65},{33,97},{65,1},{97,33},{2,66}... | collective-permute-start | bytes 786440 | tf_op jit(solution)/shard_map/ppermute | solution.py:36
  109.4 15.8 %collective-permute-start.15 = (bf16[8,128,128]{2,1,0:T(8,128)(2,1)S(1)}, bf16[8,128,128]{2,1,0:T(8,128)(2,1)}, u32[]{:S(2)}, u32[]{:S(2)}) collective-permute-start(bf16[8,128,128]{2,1,0:T(8,128)(2,1)S(1)} %copy-done.13), channel_id=1, source_target_pairs={{0,96},{32,0},{64,32},{96,64},{1,97},{33,1},{65,33},{97,65},{2,98}... | collective-permute-start | bytes 786440 | tf_op jit(solution)/shard_map/ppermute | solution.py:36
  112.6 12.6 %collective-permute-start.14 = (bf16[8,128,128]{2,1,0:T(8,128)(2,1)S(1)}, bf16[8,128,128]{2,1,0:T(8,128)(2,1)}, u32[]{:S(2)}, u32[]{:S(2)}) collective-permute-start(bf16[8,128,128]{2,1,0:T(8,128)(2,1)S(1)} %copy-done.11), channel_id=1, source_target_pairs={{0,32},{32,64},{64,96},{96,0},{1,33},{33,65},{65,97},{97,1},{2,34}... | collective-permute-start | bytes 786440 | tf_op jit(solution)/shard_map/ppermute | solution.py:36
  120.0 14.6 %all-to-all-start.4 = ((bf16[16,128,128]{2,1,0:T(8,128)(2,1)}), bf16[16,128,128]{2,1,0:T(8,128)(2,1)}, u32[]{:S(2)}, u32[]{:S(2)}) async-start(bf16[16,128,128]{2,1,0:T(8,128)(2,1)} %add_convert_fusion), calls=%async_computation.4 | async-start | bytes 1048576 | tf_op jit(solution)/shard_map/all_to_all | solution.py:45
  126.5 19.4 %collective-permute-start.19 = (bf16[128,2048]{1,0:T(8,128)(2,1)S(1)}, bf16[128,2048]{1,0:T(8,128)(2,1)S(1)}, u32[]{:S(2)}, u32[]{:S(2)}) collective-permute-start(bf16[128,2048]{1,0:T(8,128)(2,1)S(1)} %copy_bitcast_fusion.1.k0), channel_id=1, source_target_pairs={{0,96},{32,0},{64,32},{96,64},{1,97},{33,1},{65,33},{97,65},{2,98}... | collective-permute-start | bytes 1572872 | tf_op jit(solution)/shard_map/ppermute | solution.py:36
  135.8 16.0 %collective-permute-start.24 = (bf16[128,2048]{1,0:T(8,128)(2,1)S(1)}, bf16[128,2048]{1,0:T(8,128)(2,1)S(1)}, u32[]{:S(2)}, u32[]{:S(2)}) collective-permute-start(bf16[128,2048]{1,0:T(8,128)(2,1)S(1)} %copy_bitcast_fusion.v0), channel_id=1, source_target_pairs={{0,32},{32,64},{64,96},{96,0},{1,33},{33,65},{65,97},{97,1},{2,34}... | collective-permute-start | bytes 1572872 | tf_op jit(solution)/shard_map/ppermute | solution.py:36
  138.0 13.8 %all-to-all-start.2 = ((bf16[16,64,128]{2,1,0:T(8,128)(2,1)}), bf16[16,64,128]{2,1,0:T(8,128)(2,1)S(1)}, u32[]{:S(2)}, u32[]{:S(2)}) async-start(bf16[16,64,128]{2,1,0:T(8,128)(2,1)} %maximum_select_fusion), calls=%async_computation.2 | async-start | bytes 524288 | tf_op jit(solution)/shard_map/all_to_all | solution.py:45
  141.6 21.5 %collective-permute-start.21 = (bf16[128,2048]{1,0:T(8,128)(2,1)S(1)}, bf16[128,2048]{1,0:T(8,128)(2,1)S(1)}, u32[]{:S(2)}, u32[]{:S(2)}) collective-permute-start(bf16[128,2048]{1,0:T(8,128)(2,1)S(1)} %copy_bitcast_fusion.1.k0), channel_id=1, source_target_pairs={{0,32},{32,64},{64,96},{96,0},{1,33},{33,65},{65,97},{97,1},{2,34}... | collective-permute-start | bytes 1572872 | tf_op jit(solution)/shard_map/ppermute | solution.py:36
  142.6 20.5 %collective-permute-start.23 = (bf16[128,2048]{1,0:T(8,128)(2,1)S(1)}, bf16[128,2048]{1,0:T(8,128)(2,1)S(1)}, u32[]{:S(2)}, u32[]{:S(2)}) collective-permute-start(bf16[128,2048]{1,0:T(8,128)(2,1)S(1)} %copy_bitcast_fusion.v0), channel_id=1, source_target_pairs={{0,96},{32,0},{64,32},{96,64},{1,97},{33,1},{65,33},{97,65},{2,98}... | collective-permute-start | bytes 1572872 | tf_op jit(solution)/shard_map/ppermute | solution.py:36
  145.9 24.6 %collective-permute-start.20 = (bf16[128,2048]{1,0:T(8,128)(2,1)S(1)}, bf16[128,2048]{1,0:T(8,128)(2,1)}, u32[]{:S(2)}, u32[]{:S(2)}) collective-permute-start(bf16[128,2048]{1,0:T(8,128)(2,1)S(1)} %collective-permute-done.19.k1), channel_id=1, source_target_pairs={{0,96},{32,0},{64,32},{96,64},{1,97},{33,1},{65,33},{97,65},{2,98}... | collective-permute-start | bytes 1572872 | tf_op jit(solution)/shard_map/ppermute | solution.py:36
  151.8 20.1 %collective-permute-start.25 = (bf16[128,2048]{1,0:T(8,128)(2,1)S(1)}, bf16[128,2048]{1,0:T(8,128)(2,1)}, u32[]{:S(2)}, u32[]{:S(2)}) collective-permute-start(bf16[128,2048]{1,0:T(8,128)(2,1)S(1)} %collective-permute-done.24.v3), channel_id=1, source_target_pairs={{0,32},{32,64},{64,96},{96,0},{1,33},{33,65},{65,97},{97,1},{2,34}... | collective-permute-start | bytes 1572872 | tf_op jit(solution)/shard_map/ppermute | solution.py:36
  (27 other events, 277.6 us)
where the time goes:
time: 176 us; the launch traced here: 175 us
  starting transfers between devices  62.3 us (35%)
  waiting for transfers between devices  55.6 us (32%)
  Pallas kernels  38.9 us (22%)
  local copies, waits for them, and re-layouts  13 us (7%)
  other arithmetic  4.39 us (2%)
    ppermute x21, starting transfers between devices, over_z(): return lax.ppermute(array, 'dp', [(i, (i + shift) % NZ) for i in range(NZ)])  35.4 us
    ppermute x21, waiting for transfers between devices, over_z(): return lax.ppermute(array, 'dp', [(i, (i + shift) % NZ) for i in range(NZ)])  32.5 us
    all_to_all x5, starting transfers between devices, plane_exchange(): return lax.all_to_all(array, 'mem', 0, 0, axis_index_groups=groups)  25.7 us
    pallas_call x1, Pallas kernels, backward(): pl.pallas_call(bwd_kernel, out_shape=tuple(outs), in_specs=[smem, smem] +...  20.5 us
    all_to_all x5, waiting for transfers between devices, plane_exchange(): return lax.all_to_all(array, 'mem', 0, 0, axis_index_groups=groups)  20.3 us
    pallas_call x1, Pallas kernels, forward(): pl.pallas_call(fwd_kernel, out_shape=jax.ShapeDtypeStruct((3, NQ, DH), F3...  10.4 us
    unnamed x42, local copies, waits for them, and re-layouts  5.76 us
    pallas_call x1, Pallas kernels, make_list(): pl.pallas_call(list_kernel, out_shape=(jax.ShapeDtypeStruct((NENT + 8,),...  4.68 us
  transfers between devices with their start and end apart: 31, of which 16 were waited for; matrix products, arithmetic and copies ran while one was open for 5% of the time, Pallas kernels for 3%

commit v1 on v0

v1 whole, which is shorter than its diff:
```python
import jax
import jax.numpy as jnp
from jax import lax
from jax.experimental import pallas as pl
from jax.experimental.pallas import tpu as pltpu
from jax.sharding import PartitionSpec as P

H = 16
DH = 128
BLK = 128
TOPB = 16
NZ = 4
NCHIP = 16
QPER = 8
NQ = NZ * QPER
NB = 2 * NCHIP
NENT = NQ * TOPB
COUNT = NENT + 8
NCOPY = 2 * NZ + 2
UNROLL_F = 8
UNROLL_B = 8
SCALE = DH ** (-0.5)
BF = jnp.bfloat16
F32 = jnp.float32
MB = 1 << 20


NT = (((1,), (1,)), ((), ()))
NN = (((1,), (0,)), ((), ()))
TN = (((0,), (0,)), ((), ()))


def dot(a, b, dims):
    return lax.dot_general(a, b, dims, preferred_element_type=F32)


def over_z(array, shift):
    return lax.ppermute(array, "dp", [(i, (i + shift) % NZ) for i in range(NZ)])


def swap_cores(array):
    return lax.ppermute(array, "mem", [(i, i ^ 1) for i in range(2 * NCHIP)])


def plane_exchange(array):
    groups = [[2 * c + k for c in range(NCHIP)] for k in range(2)]
    return lax.all_to_all(array, "mem", 0, 0, axis_index_groups=groups)


def prepare_kernel(place, lists, queries, grads, keys, values, q, g, kv, sems):
    z, c, k = place[0], place[1], place[2]
    cols = pl.ds(pl.multiple_of(c * DH, DH), DH)
    pairs = []
    for i in range(QPER):
        rows = pl.ds(pl.multiple_of((k * QPER + i) * BLK, BLK), BLK)
        pairs.append((queries.at[rows, cols], q.at[i]))
        pairs.append((grads.at[rows, cols], g.at[i]))
    rows = pl.ds(pl.multiple_of(z * BLK, BLK), BLK)
    for h in range(H):
        cols = slice(h * DH, (h + 1) * DH)
        pairs.append((keys.at[rows, cols], kv.at[h, :BLK]))
        pairs.append((values.at[rows, cols], kv.at[h, BLK:]))
    copies = [pltpu.make_async_copy(a, b, sems.at[n]) for n, (a, b) in enumerate(pairs)]
    for copy in copies:
        copy.start()
    q[QPER, :TOPB, :TOPB] = lists[...].astype(F32).astype(BF)
    for copy in copies:
        copy.wait()


def prepare(place, queries, grads, keys, values, lists):
    smem = pl.BlockSpec(memory_space=pltpu.SMEM)
    vmem = pl.BlockSpec(memory_space=pltpu.VMEM)
    hbm = pl.BlockSpec(memory_space=pltpu.HBM)
    return pl.pallas_call(
        prepare_kernel,
        out_shape=(
            jax.ShapeDtypeStruct((QPER + 1, BLK, DH), BF),
            jax.ShapeDtypeStruct((QPER, BLK, DH), BF),
            jax.ShapeDtypeStruct((H, 2 * BLK, DH), BF),
        ),
        in_specs=[smem, vmem] + [hbm] * 4,
        out_specs=(vmem, vmem, vmem),
        scratch_shapes=[pltpu.SemaphoreType.DMA((2 * QPER + 2 * H,))],
        compiler_params=pltpu.CompilerParams(vmem_limit_bytes=60 * MB),
        name="prepare",
    )(place, lists, queries, grads, keys, values)


def list_kernel(place, l0, l1, l2, l3, home, ents):
    z = place[0]
    k = place[2]

    def group(r, lists, n):
        def block(i, n):
            q = r * QPER + i
            seen = jnp.int32(0)
            for t in range(TOPB):
                slot = home[lists[k * QPER + i, t]]
                mine = (slot & 3) == z
                owner = slot >> 2
                b = ((owner & 1) ^ k) * NCHIP + (owner >> 1)
                ents[n] = (q << 15) | ((seen * NQ + q) << 5) | b
                step = mine.astype(jnp.int32)
                n = n + step
                seen = seen + step
            return n

        return lax.fori_loop(0, QPER, block, n)

    n = jnp.int32(0)
    for r, lists in enumerate((l0, l1, l2, l3)):
        n = group(r, lists, n)
    for u in range(8):
        ents[n + u] = (NQ << 15) | (NENT << 5)
    ents[COUNT] = n


def make_list(place, lists, home):
    smem = pl.BlockSpec(memory_space=pltpu.SMEM)
    return pl.pallas_call(
        list_kernel,
        out_shape=jax.ShapeDtypeStruct((COUNT + 8,), jnp.int32),
        in_specs=[smem] * 6,
        out_specs=smem,
        name="entry_list",
    )(place, *lists, home)


def fetch(qrefs, grefs, kvrefs, qs, gs, kv, sems):
    pairs = [(ref, kv.at[p]) for p, ref in enumerate(kvrefs)]
    pairs += [(ref.at[:QPER], qs.at[r]) for r, ref in enumerate(qrefs)]
    pairs += [(ref, gs.at[r]) for r, ref in enumerate(grefs)]
    copies = [pltpu.make_async_copy(a, b, sems.at[n]) for n, (a, b) in enumerate(pairs)]
    for copy in copies:
        copy.start()
    return copies


def unpack(p):
    q = p >> 15
    b = p & 31
    return (q >> 3) & 3, q & 7, q, (p >> 5) & 1023, b >> 4, b & 15


def fwd_kernel(ents, q0, q1, q2, q3, g0, g1, g2, g3, kva, kvb, out, qs, gs, kv, st, sems):
    copies = fetch((q0, q1, q2, q3), (g0, g1, g2, g3), (kva, kvb), qs, gs, kv, sems)
    st[0] = jnp.full((NENT + 8, DH), -1e30, F32)
    st[1] = jnp.zeros((NENT + 8, DH), F32)
    st[2] = jnp.zeros((NENT + 8, DH), F32)
    for copy in copies:
        copy.wait()

    def body(n, carry):
        parts = [unpack(ents[UNROLL_F * n + u]) for u in range(UNROLL_F)]
        scores = [dot(kv[p[4], p[5], :BLK], qs[p[0], p[1]], NT) * SCALE for p in parts]
        dprob = [dot(kv[p[4], p[5], BLK:], gs[p[0], p[1]], NT) for p in parts]
        highs = [jnp.max(x, axis=0, keepdims=True) for x in scores]
        expo = [jnp.exp(x - high) for x, high in zip(scores, highs)]
        for p, high, e, d in zip(parts, highs, expo, dprob):
            row = pl.ds(p[3], 1)
            st[0, row, :] = high
            st[1, row, :] = jnp.sum(e, axis=0, keepdims=True)
            st[2, row, :] = jnp.sum(e.astype(BF).astype(F32) * d, axis=0, keepdims=True)
        return carry

    lax.fori_loop(0, (ents[COUNT] + UNROLL_F - 1) // UNROLL_F, body, 0)
    high = st[0, 0:NQ]
    for e in range(1, TOPB):
        high = jnp.maximum(high, st[0, e * NQ : (e + 1) * NQ])
    total = jnp.zeros((NQ, DH), F32)
    prod = jnp.zeros((NQ, DH), F32)
    for e in range(TOPB):
        rows = slice(e * NQ, (e + 1) * NQ)
        weight = jnp.exp(st[0, rows] - high)
        total = total + weight * st[1, rows]
        prod = prod + weight * st[2, rows]
    out[0] = high
    out[1] = total
    out[2] = prod


def scratch_in():
    return [
        pltpu.VMEM((NZ, QPER, BLK, DH), BF),
        pltpu.VMEM((NZ, QPER, BLK, DH), BF),
        pltpu.VMEM((2, NCHIP, 2 * BLK, DH), BF),
    ]


def forward(ents, xparts, kvs):
    smem = pl.BlockSpec(memory_space=pltpu.SMEM)
    far = pl.BlockSpec(memory_space=pl.ANY)
    return pl.pallas_call(
        fwd_kernel,
        out_shape=jax.ShapeDtypeStruct((3, NQ, DH), F32),
        in_specs=[smem] + [far] * 10,
        out_specs=pl.BlockSpec(memory_space=pltpu.VMEM),
        scratch_shapes=scratch_in()
        + [pltpu.VMEM((3, NENT + 8, DH), F32), pltpu.SemaphoreType.DMA((NCOPY,))],
        compiler_params=pltpu.CompilerParams(vmem_limit_bytes=14 * MB),
        name="forward",
    )(ents, *xparts, *kvs)


def bwd_kernel(
    ents, s0, s1, s2, s3, q0, q1, q2, q3, g0, g1, g2, g3, kva, kvb,
    dq0, dq1, dq2, dq3, own, other,
    qs, gs, kv, dq, dkv, away, dqs, lse, delta, sems, outsems,
):
    copies = fetch((q0, q1, q2, q3), (g0, g1, g2, g3), (kva, kvb), qs, gs, kv, sems)

    def clear(i, carry):
        zero = jnp.zeros((BLK, DH), F32)
        dq[i] = zero
        dkv[i, :BLK] = zero
        dkv[i, BLK:] = zero
        return carry

    lax.fori_loop(0, NQ, clear, 0)
    for r in range(NZ):
        rows = slice(r * QPER, (r + 1) * QPER)
        parts = []
        for ref, shift in ((s0, 0), (s1, 1), (s2, 2), (s3, 3)):
            at = (r + shift) % NZ
            parts.append([ref[n, at * QPER : (at + 1) * QPER] for n in range(3)])
        high = jnp.maximum(
            jnp.maximum(parts[0][0], parts[1][0]), jnp.maximum(parts[2][0], parts[3][0])
        )
        total = jnp.zeros((QPER, DH), F32)
        prod = jnp.zeros((QPER, DH), F32)
        for part in parts:
            weight = jnp.exp(part[0] - high)
            total = total + weight * part[1]
            prod = prod + weight * part[2]
        lse[rows] = high + jnp.log(total)
        delta[rows] = prod / total
    for copy in copies:
        copy.wait()

    lse[NQ : NQ + 8] = jnp.full((8, DH), 1e30, F32)
    delta[NQ : NQ + 8] = jnp.zeros((8, DH), F32)

    def body(n, carry):
        parts = [unpack(ents[UNROLL_B * n + u]) for u in range(UNROLL_B)]
        keys = [kv[p[4], p[5], :BLK] for p in parts]
        quer = [qs[p[0], p[1]] for p in parts]
        grad = [gs[p[0], p[1]] for p in parts]
        scores = [dot(a, b, NT) * SCALE for a, b in zip(keys, quer)]
        dprob = [dot(kv[p[4], p[5], BLK:], b, NT) for p, b in zip(parts, grad)]
        probs = [jnp.exp(x - lse[pl.ds(p[2], 1), :]) for x, p in zip(scores, parts)]
        dscore = [
            (x * (d - delta[pl.ds(p[2], 1), :]) * SCALE).astype(BF)
            for x, d, p in zip(probs, dprob, parts)
        ]
        gv = [dot(x.astype(BF), b, NN) for x, b in zip(probs, grad)]
        gk = [dot(x, b, NN) for x, b in zip(dscore, quer)]
        gq = [dot(x, b, TN) for x, b in zip(dscore, keys)]
        for p, a, b, c in zip(parts, gv, gk, gq):
            at = p[4] * NCHIP + p[5]
            dkv[at, BLK:] += a
            dkv[at, :BLK] += b
            dq[p[0] * QPER + p[1]] += c
        return carry

    lax.fori_loop(0, (ents[COUNT] + UNROLL_B - 1) // UNROLL_B, body, 0)
    away[...] = dkv[NCHIP:].astype(BF)
    sends = [pltpu.make_async_copy(away, other, outsems.at[0])]
    sends[0].start()
    sends.append(pltpu.make_async_copy(dkv.at[:NCHIP], own, outsems.at[1]))
    sends.append(pltpu.make_async_copy(dq.at[:QPER], dq0, outsems.at[2]))
    sends[1].start()
    sends[2].start()
    dqs[...] = dq[QPER:].astype(BF)
    for r, ref in enumerate((dq1, dq2, dq3)):
        part = dqs.at[r * QPER : (r + 1) * QPER]
        sends.append(pltpu.make_async_copy(part, ref, outsems.at[3 + r]))
        sends[-1].start()
    for send in sends:
        send.wait()


def backward(ents, stats, xparts, kvs):
    smem = pl.BlockSpec(memory_space=pltpu.SMEM)
    vmem = pl.BlockSpec(memory_space=pltpu.VMEM)
    far = pl.BlockSpec(memory_space=pl.ANY)
    tile = (BLK, DH)
    outs = [jax.ShapeDtypeStruct((QPER,) + tile, F32)]
    outs += [jax.ShapeDtypeStruct((QPER,) + tile, BF)] * 3
    pair = (NCHIP, 2 * BLK, DH)
    outs += [jax.ShapeDtypeStruct(pair, F32), jax.ShapeDtypeStruct(pair, BF)]
    return pl.pallas_call(
        bwd_kernel,
        out_shape=tuple(outs),
        in_specs=[smem] + [vmem] * 4 + [far] * 10,
        out_specs=tuple([far] * 6),
        scratch_shapes=scratch_in()
        + [
            pltpu.VMEM((NQ,) + tile, F32),
            pltpu.VMEM((NB, 2 * BLK, DH), F32),
            pltpu.VMEM(pair, BF),
            pltpu.VMEM((NQ - QPER,) + tile, BF),
            pltpu.VMEM((NQ + 8, DH), F32),
            pltpu.VMEM((NQ + 8, DH), F32),
            pltpu.SemaphoreType.DMA((NCOPY,)),
            pltpu.SemaphoreType.DMA((6,)),
        ],
        compiler_params=pltpu.CompilerParams(vmem_limit_bytes=24 * MB),
        name="backward",
    )(ents, *stats, *xparts, *kvs)


def place_parts(z, parts, sems):
    copies = []
    for n, (r, ref, out) in enumerate(parts):
        rows = pl.ds(pl.multiple_of(((z + r) & 3) * BLK, BLK), BLK)
        copies.append(pltpu.make_async_copy(ref, out.at[rows], sems.at[n]))
    for copy in copies:
        copy.start()
    for copy in copies:
        copy.wait()


def near_kernel(place, k0, k1, k3, v0, v1, v3, outk, outv, sems):
    parts = [(0, k0, outk), (1, k1, outk), (3, k3, outk)]
    parts += [(0, v0, outv), (1, v1, outv), (3, v3, outv)]
    place_parts(place[0], parts, sems)


def far_kernel(place, k2, v2, ink, inv, outk, outv, sems):
    place_parts(place[0], [(2, k2, outk), (2, v2, outv)], sems)


def place_near(place, kparts, vparts):
    smem = pl.BlockSpec(memory_space=pltpu.SMEM)
    vmem = pl.BlockSpec(memory_space=pltpu.VMEM)
    far = pl.BlockSpec(memory_space=pl.ANY)
    shape = jax.ShapeDtypeStruct((NZ * BLK, H * DH), BF)
    return pl.pallas_call(
        near_kernel,
        out_shape=(shape, shape),
        in_specs=[smem] + [vmem] * 6,
        out_specs=(far, far),
        scratch_shapes=[pltpu.SemaphoreType.DMA((6,))],
        compiler_params=pltpu.CompilerParams(vmem_limit_bytes=16 * MB),
        name="place_near",
    )(place, *kparts, *vparts)


def place_far(place, near, k_far, v_far):
    smem = pl.BlockSpec(memory_space=pltpu.SMEM)
    vmem = pl.BlockSpec(memory_space=pltpu.VMEM)
    far = pl.BlockSpec(memory_space=pl.ANY)
    shape = jax.ShapeDtypeStruct((NZ * BLK, H * DH), BF)
    return pl.pallas_call(
        far_kernel,
        out_shape=(shape, shape),
        in_specs=[smem, vmem, vmem, far, far],
        out_specs=(far, far),
        scratch_shapes=[pltpu.SemaphoreType.DMA((2,))],
        input_output_aliases={3: 0, 4: 1},
        compiler_params=pltpu.CompilerParams(vmem_limit_bytes=16 * MB),
        name="place_far",
    )(place, k_far, v_far, *near)


def heads_first(array):
    return jnp.transpose(array.reshape(array.shape[0], H, DH), (1, 0, 2))


def rows_first(array):
    return jnp.transpose(array, (1, 0, 2)).reshape(array.shape[1], H * DH)


def per_device(queries, grad_out, mem_keys, mem_values, block_lists, block_home):
    z = lax.axis_index("dp")
    m = lax.axis_index("mem")
    c, k = m // 2, m % 2
    place = jnp.stack([z, c, k]).astype(jnp.int32)

    q_own, g_own, kv_cat = prepare(place, queries, grad_out, mem_keys, mem_values, block_lists)
    kv_cat, l_far = lax.optimization_barrier((kv_cat, over_z(block_lists, 2)))
    q_prev = over_z(q_own, 1)
    g_next = over_z(g_own, -1)
    g_prev = over_z(g_own, 1)
    q_next = over_z(q_own, -1)
    kv_own, q_prev, g_next, g_prev, q_next = lax.optimization_barrier(
        (plane_exchange(kv_cat), q_prev, g_next, g_prev, q_next)
    )
    q_far = over_z(q_prev, 1)
    g_far = over_z(g_next, -1)
    kvs = (kv_own, swap_cores(kv_own))
    l_prev = q_prev[QPER, :TOPB, :TOPB].astype(jnp.int32)
    l_next = q_next[QPER, :TOPB, :TOPB].astype(jnp.int32)
    ents = make_list(place, (block_lists, l_next, l_far, l_prev), block_home)
    xparts = (q_own, q_next, q_far, q_prev, g_own, g_next, g_far, g_prev)

    stat = forward(ents, xparts, kvs)
    stats = (stat, over_z(stat, 1), over_z(stat, 2), over_z(stat, -1))
    dq0, dq1, dq2, dq3, own, other = backward(ents, stats, xparts, kvs)

    both = (own + swap_cores(other).astype(F32)).astype(BF)
    got = plane_exchange(both)
    k_own, v_own = rows_first(got[:, :BLK]), rows_first(got[:, BLK:])
    v_prev = over_z(v_own, 1)
    v_next = over_z(v_own, -1)
    k_next = over_z(k_own, -1)
    k_prev = over_z(k_own, 1)
    v_far = over_z(v_prev, 1)
    k_far = over_z(k_next, -1)
    near = place_near(place, (k_own, k_next, k_prev), (v_own, v_next, v_prev))
    grad_keys, grad_values = place_far(place, near, k_far, v_far)

    dq_sum = (
        dq0
        + over_z(dq1, 1).astype(F32)
        + over_z(dq3, -1).astype(F32)
        + over_z(dq2, 2).astype(F32)
    ).astype(BF)
    half = BLK // 2
    keep = lax.dynamic_slice_in_dim(dq_sum, k * half, half, 1)
    give = lax.dynamic_slice_in_dim(dq_sum, (1 - k) * half, half, 1)
    got = swap_cores(give)
    whole = jnp.where(
        k == 0, jnp.concatenate([keep, got], axis=0), jnp.concatenate([got, keep], axis=0)
    )
    grad_queries = rows_first(plane_exchange(whole))
    return grad_queries, grad_keys, grad_values


def solution(mesh):
    in_specs = (P("dp", None), P("dp", None), P("mem", None), P("mem", None), P("dp", None), P())
    out_specs = (P(("dp", "mem"), None), P("mem", None), P("mem", None))
    return jax.shard_map(
        per_device, mesh=mesh, in_specs=in_specs, out_specs=out_specs, check_vma=False
    )
```

time: 176 us -> 154 us (0.88); the launches traced: 175 us -> 151 us
  starting transfers between devices: 62.3 us -> 48 us
  local copies, waits for them, and re-layouts: 13 us -> 8.03 us
  waiting for transfers between devices: 55.6 us -> 51.4 us
    all_to_all x5 -> x3, waiting for transfers between devices: 20.3 us -> 6.69 us  [plane_exchange(): return lax.all_to_all(array, 'mem', 0, 0, axis_index_groups=groups)]
    ppermute x21 -> x19, waiting for transfers between devices: 32.5 us -> 40.8 us  [over_z(): return lax.ppermute(array, 'dp', [(i, (i + shift) % NZ) for i in range(NZ)])]
    all_to_all x5 -> x3, starting transfers between devices: 25.7 us -> 18.9 us  [plane_exchange(): return lax.all_to_all(array, 'mem', 0, 0, axis_index_groups=groups)]
    ppermute x21 -> x19, starting transfers between devices: 35.4 us -> 29.1 us  [over_z(): return lax.ppermute(array, 'dp', [(i, (i + shift) % NZ) for i in range(NZ)])]
    dynamic_slice x4 -> x0, local copies, waits for them, and re-layouts: 3.21 us -> none  [the longest x1 1.27 us: per_device(): vz = heads_first(lax.dynamic_slice_in_dim(mem_values, z * BLK, BLK, 0))]
    reshape x2 -> x0, local copies, waits for them, and re-layouts: 2.07 us -> none  [heads_first(): return jnp.transpose(array.reshape(array.shape[0], H, DH), (1, 0, 2))]
    unnamed x42 -> x41, local copies, waits for them, and re-layouts: 5.76 us -> 7.01 us
    ppermute x5 -> x3, waiting for transfers between devices: 2.74 us -> 3.99 us  [swap_cores(): return lax.ppermute(array, 'mem', [(i, i ^ 1) for i in range(2 * NCHIP)])]
  transfers between devices with their start and end apart: 31 -> 25, of which waited for: 16 -> 15; matrix products, arithmetic and copies ran while one was open for 5% -> 2% of each run, Pallas kernels for 3% -> 7%
where the time goes in v1:
time: 154 us; the launch traced here: 151 us
  waiting for transfers between devices  51.4 us (33%)
  starting transfers between devices  48 us (31%)
  Pallas kernels  39.5 us (26%)
  local copies, waits for them, and re-layouts  8.03 us (5%)
  other arithmetic  3.41 us (2%)
    ppermute x19, waiting for transfers between devices, over_z(): return lax.ppermute(array, 'dp', [(i, (i + shift) % NZ) for i in range(NZ)])  40.8 us
    ppermute x19, starting transfers between devices, over_z(): return lax.ppermute(array, 'dp', [(i, (i + shift) % NZ) for i in range(NZ)])  29.1 us
    all_to_all x3, starting transfers between devices, plane_exchange(): return lax.all_to_all(array, 'mem', 0, 0, axis_index_groups=groups)  18.9 us
    pallas_call x1, Pallas kernels, backward(): pl.pallas_call(bwd_kernel, out_shape=tuple(outs), in_specs=[smem] + [vmem...  15.5 us
    pallas_call x1, Pallas kernels, forward(): pl.pallas_call(fwd_kernel, out_shape=jax.ShapeDtypeStruct((3, NQ, DH), F3...  10.9 us
    unnamed x41, local copies, waits for them, and re-layouts  7.01 us
    all_to_all x3, waiting for transfers between devices, plane_exchange(): return lax.all_to_all(array, 'mem', 0, 0, axis_index_groups=groups)  6.69 us
    pallas_call x1, Pallas kernels, make_list(): pl.pallas_call(list_kernel, out_shape=jax.ShapeDtypeStruct((COUNT + 8,),...  5.03 us
  transfers between devices with their start and end apart: 25, of which 15 were waited for; matrix products, arithmetic and copies ran while one was open for 2% of the time, Pallas kernels for 7%

profile of v1, /device:TPU:0, one launch (start us, length us, event | category | flops | bytes accessed | tf_op | source)
XLA Modules:
  0.0 151.3 jit_solution(5922688686406740349)
XLA Ops:
  0.6 4.0 %collective-permute-start = (s32[16,16]{1,0:T(8,128)}, s32[16,16]{1,0:T(8,128)S(1)}, u32[]{:S(2)}, u32[]{:S(2)}) collective-permute-start(s32[16,16]{1,0:T(8,128)} %l0.1), channel_id=1, source_target_pairs={{0,64},{32,96},{64,0},{96,32},{1,65},{33,97},{65,1},{97,33},{2,66}... | collective-permute-start | bytes 3080 | tf_op jit(solution)/shard_map/ppermute | solution.py:38
  5.3 3.7 %prepare.1 = (bf16[9,128,128]{2,1,0:T(8,128)(2,1)}, bf16[8,128,128]{2,1,0:T(8,128)(2,1)}, bf16[16,256,128]{2,1,0:T(8,128)(2,1)}) custom-call(s32[3]{0:T(128)} %pad_add_fusion.place, s32[16,16]{1,0:T(8,128)} %l0.1, bf16[2048,2048]{1,0:T(8,128)(2,1)} %queries.1, bf16[2048,2048]{1,0:T(8,128)(2,1)} %grads.1, bf16[512,2048]{1,0:T(8,128)(2,1)} %keys.1, ...), custom_call_target="tpu_custom_call" | custom-call | tf_op jit(solution)/shard_map/prepare/pallas_call | solution.py:75
  9.0 7.2 %all-to-all-start = ((bf16[16,256,128]{2,1,0:T(8,128)(2,1)}), bf16[16,256,128]{2,1,0:T(8,128)(2,1)S(1)}, u32[]{:S(2)}, u32[]{:S(2)}) async-start(bf16[16,256,128]{2,1,0:T(8,128)(2,1)} %get-tuple-element.24), calls=%async_computation | async-start | bytes 2097152 | tf_op jit(solution)/shard_map/all_to_all | solution.py:47
  19.3 2.2 %collective-permute-start.2 = (bf16[8,128,128]{2,1,0:T(8,128)(2,1)S(1)}, bf16[8,128,128]{2,1,0:T(8,128)(2,1)S(1)}, u32[]{:S(2)}, u32[]{:S(2)}) collective-permute-start(bf16[8,128,128]{2,1,0:T(8,128)(2,1)S(1)} %copy-done.1), channel_id=1, source_target_pairs={{0,96},{32,0},{64,32},{96,64},{1,97},{33,1},{65,33},{97,65},{2,98}... | collective-permute-start | bytes 786440 | tf_op jit(solution)/shard_map/ppermute | solution.py:38
  21.6 10.2 %collective-permute-done.3.g3 = bf16[8,128,128]{2,1,0:T(8,128)(2,1)S(1)} collective-permute-done((bf16[8,128,128]{2,1,0:T(8,128)(2,1)S(1)}, bf16[8,128,128]{2,1,0:T(8,128)(2,1)S(1)}, u32[]{:S(2)}, u32[]{:S(2)}) %collective-permute-start.3) | collective-permute-done | bytes 262176 | tf_op jit(solution)/shard_map/ppermute | solution.py:38
  34.5 2.2 %collective-permute-start.6 = (bf16[8,128,128]{2,1,0:T(8,128)(2,1)}, bf16[8,128,128]{2,1,0:T(8,128)(2,1)}, u32[]{:S(2)}, u32[]{:S(2)}) collective-permute-start(bf16[8,128,128]{2,1,0:T(8,128)(2,1)} %copy-done.5), channel_id=1, source_target_pairs={{0,96},{32,0},{64,32},{96,64},{1,97},{33,1},{65,33},{97,65},{2,98}... | collective-permute-start | bytes 786440 | tf_op jit(solution)/shard_map/ppermute | solution.py:38
  37.3 5.0 %entry_list.1.ents = s32[528]{0:T(1024)} custom-call(s32[3]{0:T(128)} %pad_add_fusion.place, s32[16,16]{1,0:T(8,128)} %l0.1, s32[16,16]{1,0:T(8,128)} %get-tuple-element.48.l1, s32[16,16]{1,0:T(8,128)} %copy-done.19, s32[16,16]{1,0:T(8,128)} %get-tuple-element.47.l3, s32[128]{0:T(128)} %home.1), custom_call_target="tpu_custom_call" | custom-call | tf_op jit(solution)/shard_map/entry_list/pallas_call | solution.py:121
  46.7 10.9 %forward.1.s0 = f32[3,32,128]{2,1,0:T(8,128)S(1)} custom-call(s32[528]{0:T(1024)S(1)} %copy-done.10, bf16[9,128,128]{2,1,0:T(8,128)(2,1)S(1)} %copy-done, bf16[9,128,128]{2,1,0:T(8,128)(2,1)S(1)} %collective-permute-done.4.q1, bf16[9,128,128]{2,1,0:T(8,128)(2,1)S(1)} %collective-permute-done.5.q2, bf16[9,128,128]{2,1,0:T(8,128)(2,1)S(1)} %collective-permute-done.1.q3, ...), custom_call_target="tpu_custom_call" | custom-call | tf_op jit(solution)/shard_map/forward/pallas_call | solution.py:194
  57.7 2.7 %collective-permute-start.9 = (f32[3,32,128]{2,1,0:T(8,128)S(1)}, f32[3,32,128]{2,1,0:T(8,128)S(1)}, u32[]{:S(2)}, u32[]{:S(2)}) collective-permute-start(f32[3,32,128]{2,1,0:T(8,128)S(1)} %forward.1.s0), channel_id=1, source_target_pairs={{0,64},{32,96},{64,0},{96,32},{1,65},{33,97},{65,1},{97,33},{2,66}... | collective-permute-start | bytes 147464 | tf_op jit(solution)/shard_map/ppermute | solution.py:38
  63.7 2.0 %collective-permute-done.8.s1 = f32[3,32,128]{2,1,0:T(8,128)S(1)} collective-permute-done((f32[3,32,128]{2,1,0:T(8,128)S(1)}, f32[3,32,128]{2,1,0:T(8,128)S(1)}, u32[]{:S(2)}, u32[]{:S(2)}) %collective-permute-start.8) | collective-permute-done | bytes 49184 | tf_op jit(solution)/shard_map/ppermute | solution.py:38
  65.7 15.5 %backward.1 = (f32[8,128,128]{2,1,0:T(8,128)S(1)}, bf16[8,128,128]{2,1,0:T(8,128)(2,1)S(1)}, bf16[8,128,128]{2,1,0:T(8,128)(2,1)S(1)}, bf16[8,128,128]{2,1,0:T(8...) custom-call(s32[528]{0:T(1024)S(1)} %copy-done.11, f32[3,32,128]{2,1,0:T(8,128)S(1)} %forward.1.s0, ...), custom_call_target="tpu_custom_call" | custom-call | tf_op jit(solution)/shard_map/backward/pallas_call | solution.py:292
  84.1 2.7 %collective-permute-done.15 = bf16[16,256,128]{2,1,0:T(8,128)(2,1)S(1)} collective-permute-done((bf16[16,256,128]{2,1,0:T(8,128)(2,1)S(1)}, bf16[16,256,128]{2,1,0:T(8,128)(2,1)S(1)}, u32[]{:S(2)}, u32[]{:S(2)}) %collective-permute-start.15) | collective-permute-done | bytes 1048608 | tf_op jit(solution)/shard_map/ppermute | solution.py:42
  88.0 6.8 %all-to-all-start.2 = ((bf16[16,256,128]{2,1,0:T(8,128)(2,1)}), bf16[16,256,128]{2,1,0:T(8,128)(2,1)S(1)}, u32[]{:S(2)}, u32[]{:S(2)}) async-start(bf16[16,256,128]{2,1,0:T(8,128)(2,1)} %add_convert_fusion), calls=%async_computation.2 | async-start | bytes 2097152 | tf_op jit(solution)/shard_map/all_to_all | solution.py:47
  94.9 3.2 %collective-permute-start.12 = (bf16[8,128,128]{2,1,0:T(8,128)(2,1)S(1)}, bf16[8,128,128]{2,1,0:T(8,128)(2,1)S(1)}, u32[]{:S(2)}, u32[]{:S(2)}) collective-permute-start(bf16[8,128,128]{2,1,0:T(8,128)(2,1)S(1)} %copy-done.16), channel_id=1, source_target_pairs={{0,96},{32,0},{64,32},{96,64},{1,97},{33,1},{65,33},{97,65},{2,98}... | collective-permute-start | bytes 786440 | tf_op jit(solution)/shard_map/ppermute | solution.py:38
  99.7 10.0 %collective-permute-done.11 = bf16[8,128,128]{2,1,0:T(8,128)(2,1)S(1)} collective-permute-done((bf16[8,128,128]{2,1,0:T(8,128)(2,1)S(1)}, bf16[8,128,128]{2,1,0:T(8,128)(2,1)S(1)}, u32[]{:S(2)}, u32[]{:S(2)}) %collective-permute-start.11) | collective-permute-done | bytes 262176 | tf_op jit(solution)/shard_map/ppermute | solution.py:38
  109.9 3.0 %all-to-all-done.2 = bf16[16,256,128]{2,1,0:T(8,128)(2,1)S(1)} async-done(((bf16[16,256,128]{2,1,0:T(8,128)(2,1)}), bf16[16,256,128]{2,1,0:T(8,128)(2,1)S(1)}, u32[]{:S(2)}, u32[]{:S(2)}) %all-to-all-start.2) | async-done | bytes 1048608 | tf_op jit(solution)/shard_map/all_to_all | solution.py:47
  113.4 2.0 %collective-permute-start.18 = (bf16[128,2048]{1,0:T(8,128)(2,1)S(1)}, bf16[128,2048]{1,0:T(8,128)(2,1)S(1)}, u32[]{:S(2)}, u32[]{:S(2)}) collective-permute-start(bf16[128,2048]{1,0:T(8,128)(2,1)S(1)} %bitcast.27), channel_id=1, source_target_pairs={{0,32},{32,64},{64,96},{96,0},{1,33},{33,65},{65,97},{97,1},{2,34}... | collective-permute-start | bytes 1572872 | tf_op jit(solution)/shard_map/ppermute | solution.py:38
  117.6 4.9 %all-to-all-start.1 = ((bf16[16,64,128]{2,1,0:T(8,128)(2,1)}), bf16[16,64,128]{2,1,0:T(8,128)(2,1)S(1)}, u32[]{:S(2)}, u32[]{:S(2)}) async-start(bf16[16,64,128]{2,1,0:T(8,128)(2,1)} %maximum_select_fusion), calls=%async_computation.1 | async-start | bytes 524288 | tf_op jit(solution)/shard_map/all_to_all | solution.py:47
  122.9 3.0 %collective-permute-start.21 = (bf16[128,2048]{1,0:T(8,128)(2,1)S(1)}, bf16[128,2048]{1,0:T(8,128)(2,1)S(1)}, u32[]{:S(2)}, u32[]{:S(2)}) collective-permute-start(bf16[128,2048]{1,0:T(8,128)(2,1)S(1)} %bitcast.28), channel_id=1, source_target_pairs={{0,96},{32,0},{64,32},{96,64},{1,97},{33,1},{65,33},{97,65},{2,98}... | collective-permute-start | bytes 1572872 | tf_op jit(solution)/shard_map/ppermute | solution.py:38
  127.9 3.4 %all-to-all-done.1 = bf16[16,64,128]{2,1,0:T(8,128)(2,1)S(1)} async-done(((bf16[16,64,128]{2,1,0:T(8,128)(2,1)}), bf16[16,64,128]{2,1,0:T(8,128)(2,1)S(1)}, u32[]{:S(2)}, u32[]{:S(2)}) %all-to-all-start.1) | async-done | bytes 262176 | tf_op jit(solution)/shard_map/all_to_all | solution.py:47
  132.1 6.5 %collective-permute-done.20.k3 = bf16[128,2048]{1,0:T(8,128)(2,1)S(1)} collective-permute-done((bf16[128,2048]{1,0:T(8,128)(2,1)S(1)}, bf16[128,2048]{1,0:T(8,128)(2,1)S(1)}, u32[]{:S(2)}, u32[]{:S(2)}) %collective-permute-start.20) | collective-permute-done | bytes 524320 | tf_op jit(solution)/shard_map/ppermute | solution.py:38
  138.6 2.3 %place_near.1 = (bf16[512,2048]{1,0:T(8,128)(2,1)}, bf16[512,2048]{1,0:T(8,128)(2,1)}) custom-call(s32[3]{0:T(128)S(1)} %copy-done.12, bf16[128,2048]{1,0:T(8,128)(2,1)S(1)} %bitcast.32, bf16[128,2048]{1,0:T(8,128)(2,1)S(1)} %collective-permute-done.16.k1, bf16[128,2048]{1,0:T(8,128)(2,1)S(1)} %collective-permute-done.20.k3, bf16[128,2048]{1,0:T(8,128)(2,1)S(1)} %bitcast.29, ...), custom_call_target="tpu_custom_call" | custom-call | tf_op jit(solution)/shard_map/place_near/pallas_call | solution.py:339
  140.8 7.5 %collective-permute-done.17.k2 = bf16[128,2048]{1,0:T(8,128)(2,1)} collective-permute-done((bf16[128,2048]{1,0:T(8,128)(2,1)S(1)}, bf16[128,2048]{1,0:T(8,128)(2,1)}, u32[]{:S(2)}, u32[]{:S(2)}) %collective-permute-start.17) | collective-permute-done | bytes 524320 | tf_op jit(solution)/shard_map/ppermute | solution.py:38
  149.1 2.2 %place_far.1 = (bf16[512,2048]{1,0:T(8,128)(2,1)}, bf16[512,2048]{1,0:T(8,128)(2,1)}) custom-call(s32[3]{0:T(128)S(1)} %copy-done.12, bf16[128,2048]{1,0:T(8,128)(2,1)} %collective-permute-done.17.k2, bf16[128,2048]{1,0:T(8,128)(2,1)} %collective-permute-done.19.v2, ...), custom_call_target="tpu_custom_call", output_to_operand_aliasing={{0}: (3, {}), {1}: (4, {})} | custom-call | tf_op jit(solution)/shard_map/place_far/pallas_call | solution.py:355
  (82 shorter events, 27.4 us)
Async XLA Ops:
  0.6 8.4 %collective-permute-start = (s32[16,16]{1,0:T(8,128)}, s32[16,16]{1,0:T(8,128)S(1)}, u32[]{:S(2)}, u32[]{:S(2)}) collective-permute-start(s32[16,16]{1,0:T(8,128)} %l0.1), channel_id=1, source_target_pairs={{0,64},{32,96},{64,0},{96,32},{1,65},{33,97},{65,1},{97,33},{2,66}... | collective-permute-start | bytes 3080 | tf_op jit(solution)/shard_map/ppermute | solution.py:38
  9.0 24.5 %all-to-all-start = ((bf16[16,256,128]{2,1,0:T(8,128)(2,1)}), bf16[16,256,128]{2,1,0:T(8,128)(2,1)S(1)}, u32[]{:S(2)}, u32[]{:S(2)}) async-start(bf16[16,256,128]{2,1,0:T(8,128)(2,1)} %get-tuple-element.24), calls=%async_computation | async-start | bytes 2097152 | tf_op jit(solution)/shard_map/all_to_all | solution.py:47
  16.2 16.2 %collective-permute-start.4 = (bf16[9,128,128]{2,1,0:T(8,128)(2,1)S(1)}, bf16[9,128,128]{2,1,0:T(8,128)(2,1)S(1)}, u32[]{:S(2)}, u32[]{:S(2)}) collective-permute-start(bf16[9,128,128]{2,1,0:T(8,128)(2,1)S(1)} %copy-done), channel_id=1, source_target_pairs={{0,96},{32,0},{64,32},{96,64},{1,97},{33,1},{65,33},{97,65},{2,98}... | collective-permute-start | bytes 884744 | tf_op jit(solution)/shard_map/ppermute | solution.py:38
  17.3 15.8 %collective-permute-start.1 = (bf16[9,128,128]{2,1,0:T(8,128)(2,1)S(1)}, bf16[9,128,128]{2,1,0:T(8,128)(2,1)S(1)}, u32[]{:S(2)}, u32[]{:S(2)}) collective-permute-start(bf16[9,128,128]{2,1,0:T(8,128)(2,1)S(1)} %copy-done), channel_id=1, source_target_pairs={{0,32},{32,64},{64,96},{96,0},{1,33},{33,65},{65,97},{97,1},{2,34}... | collective-permute-start | bytes 884744 | tf_op jit(solution)/shard_map/ppermute | solution.py:38
  18.3 13.4 %collective-permute-start.3 = (bf16[8,128,128]{2,1,0:T(8,128)(2,1)S(1)}, bf16[8,128,128]{2,1,0:T(8,128)(2,1)S(1)}, u32[]{:S(2)}, u32[]{:S(2)}) collective-permute-start(bf16[8,128,128]{2,1,0:T(8,128)(2,1)S(1)} %copy-done.1), channel_id=1, source_target_pairs={{0,32},{32,64},{64,96},{96,0},{1,33},{33,65},{65,97},{97,1},{2,34}... | collective-permute-start | bytes 786440 | tf_op jit(solution)/shard_map/ppermute | solution.py:38
  19.3 13.1 %collective-permute-start.2 = (bf16[8,128,128]{2,1,0:T(8,128)(2,1)S(1)}, bf16[8,128,128]{2,1,0:T(8,128)(2,1)S(1)}, u32[]{:S(2)}, u32[]{:S(2)}) collective-permute-start(bf16[8,128,128]{2,1,0:T(8,128)(2,1)S(1)} %copy-done.1), channel_id=1, source_target_pairs={{0,96},{32,0},{64,32},{96,64},{1,97},{33,1},{65,33},{97,65},{2,98}... | collective-permute-start | bytes 786440 | tf_op jit(solution)/shard_map/ppermute | solution.py:38
  33.5 10.6 %collective-permute-start.7 = (bf16[16,256,128]{2,1,0:T(8,128)(2,1)S(1)}, bf16[16,256,128]{2,1,0:T(8,128)(2,1)S(1)}, u32[]{:S(2)}, u32[]{:S(2)}) collective-permute-start(bf16[16,256,128]{2,1,0:T(8,128)(2,1)S(1)} %all-to-all-done.kva), channel_id=1, source_target_pairs={{0,1},{1,0},{2,3},{3,2},{4,5},{5,4},{6,7},{7,6},{8,9},{9,8},{10,11... | collective-permute-start | bytes 3145736 | tf_op jit(solution)/shard_map/ppermute | solution.py:42
  33.5 10.6 %collective-permute-start.5 = (bf16[9,128,128]{2,1,0:T(8,128)(2,1)S(1)}, bf16[9,128,128]{2,1,0:T(8,128)(2,1)S(1)}, u32[]{:S(2)}, u32[]{:S(2)}) collective-permute-start(bf16[9,128,128]{2,1,0:T(8,128)(2,1)S(1)} %collective-permute-done.1.q3), channel_id=1, source_target_pairs={{0,32},{32,64},{64,96},{96,0},{1,33},{33,65},{65,97},{97,1},{2,34}... | collective-permute-start | bytes 884744 | tf_op jit(solution)/shard_map/ppermute | solution.py:38
  34.5 8.8 %collective-permute-start.6 = (bf16[8,128,128]{2,1,0:T(8,128)(2,1)}, bf16[8,128,128]{2,1,0:T(8,128)(2,1)}, u32[]{:S(2)}, u32[]{:S(2)}) collective-permute-start(bf16[8,128,128]{2,1,0:T(8,128)(2,1)} %copy-done.5), channel_id=1, source_target_pairs={{0,96},{32,0},{64,32},{96,64},{1,97},{33,1},{65,33},{97,65},{2,98}... | collective-permute-start | bytes 786440 | tf_op jit(solution)/shard_map/ppermute | solution.py:38
  57.6 4.7 %collective-permute-start.10 = (f32[3,32,128]{2,1,0:T(8,128)S(1)}, f32[3,32,128]{2,1,0:T(8,128)S(1)}, u32[]{:S(2)}, u32[]{:S(2)}) collective-permute-start(f32[3,32,128]{2,1,0:T(8,128)S(1)} %forward.1.s0), channel_id=1, source_target_pairs={{0,96},{32,0},{64,32},{96,64},{1,97},{33,1},{65,33},{97,65},{2,98}... | collective-permute-start | bytes 147464 | tf_op jit(solution)/shard_map/ppermute | solution.py:38
  57.7 6.0 %collective-permute-start.9 = (f32[3,32,128]{2,1,0:T(8,128)S(1)}, f32[3,32,128]{2,1,0:T(8,128)S(1)}, u32[]{:S(2)}, u32[]{:S(2)}) collective-permute-start(f32[3,32,128]{2,1,0:T(8,128)S(1)} %forward.1.s0), channel_id=1, source_target_pairs={{0,64},{32,96},{64,0},{96,32},{1,65},{33,97},{65,1},{97,33},{2,66}... | collective-permute-start | bytes 147464 | tf_op jit(solution)/shard_map/ppermute | solution.py:38
  60.3 5.3 %collective-permute-start.8 = (f32[3,32,128]{2,1,0:T(8,128)S(1)}, f32[3,32,128]{2,1,0:T(8,128)S(1)}, u32[]{:S(2)}, u32[]{:S(2)}) collective-permute-start(f32[3,32,128]{2,1,0:T(8,128)S(1)} %forward.1.s0), channel_id=1, source_target_pairs={{0,32},{32,64},{64,96},{96,0},{1,33},{33,65},{65,97},{97,1},{2,34}... | collective-permute-start | bytes 147464 | tf_op jit(solution)/shard_map/ppermute | solution.py:38
  84.1 2.7 %collective-permute-start.15 = (bf16[16,256,128]{2,1,0:T(8,128)(2,1)S(1)}, bf16[16,256,128]{2,1,0:T(8,128)(2,1)S(1)}, u32[]{:S(2)}, u32[]{:S(2)}) collective-permute-start(bf16[16,256,128]{2,1,0:T(8,128)(2,1)S(1)} %get-tuple-element.38), channel_id=1, source_target_pairs={{0,1},{1,0},{2,3},{3,2},{4,5},{5,4},{6,7},{7,6},{8,9},{9,8},{10,11... | collective-permute-start | bytes 3145736 | tf_op jit(solution)/shard_map/ppermute | solution.py:42
  88.0 24.9 %all-to-all-start.2 = ((bf16[16,256,128]{2,1,0:T(8,128)(2,1)}), bf16[16,256,128]{2,1,0:T(8,128)(2,1)S(1)}, u32[]{:S(2)}, u32[]{:S(2)}) async-start(bf16[16,256,128]{2,1,0:T(8,128)(2,1)} %add_convert_fusion), calls=%async_computation.2 | async-start | bytes 2097152 | tf_op jit(solution)/shard_map/all_to_all | solution.py:47
  94.8 15.0 %collective-permute-start.11 = (bf16[8,128,128]{2,1,0:T(8,128)(2,1)S(1)}, bf16[8,128,128]{2,1,0:T(8,128)(2,1)S(1)}, u32[]{:S(2)}, u32[]{:S(2)}) collective-permute-start(bf16[8,128,128]{2,1,0:T(8,128)(2,1)S(1)} %copy-done.18), channel_id=1, source_target_pairs={{0,32},{32,64},{64,96},{96,0},{1,33},{33,65},{65,97},{97,1},{2,34}... | collective-permute-start | bytes 786440 | tf_op jit(solution)/shard_map/ppermute | solution.py:38
  94.9 14.9 %collective-permute-start.12 = (bf16[8,128,128]{2,1,0:T(8,128)(2,1)S(1)}, bf16[8,128,128]{2,1,0:T(8,128)(2,1)S(1)}, u32[]{:S(2)}, u32[]{:S(2)}) collective-permute-start(bf16[8,128,128]{2,1,0:T(8,128)(2,1)S(1)} %copy-done.16), channel_id=1, source_target_pairs={{0,96},{32,0},{64,32},{96,64},{1,97},{33,1},{65,33},{97,65},{2,98}... | collective-permute-start | bytes 786440 | tf_op jit(solution)/shard_map/ppermute | solution.py:38
  98.1 11.7 %collective-permute-start.13 = (bf16[8,128,128]{2,1,0:T(8,128)(2,1)S(1)}, bf16[8,128,128]{2,1,0:T(8,128)(2,1)S(1)}, u32[]{:S(2)}, u32[]{:S(2)}) collective-permute-start(bf16[8,128,128]{2,1,0:T(8,128)(2,1)S(1)} %copy-done.14), channel_id=1, source_target_pairs={{0,64},{32,96},{64,0},{96,32},{1,65},{33,97},{65,1},{97,33},{2,66}... | collective-permute-start | bytes 786440 | tf_op jit(solution)/shard_map/ppermute | solution.py:38
  113.3 12.6 %collective-permute-start.16 = (bf16[128,2048]{1,0:T(8,128)(2,1)S(1)}, bf16[128,2048]{1,0:T(8,128)(2,1)S(1)}, u32[]{:S(2)}, u32[]{:S(2)}) collective-permute-start(bf16[128,2048]{1,0:T(8,128)(2,1)S(1)} %bitcast.30), channel_id=1, source_target_pairs={{0,96},{32,0},{64,32},{96,64},{1,97},{33,1},{65,33},{97,65},{2,98}... | collective-permute-start | bytes 1572872 | tf_op jit(solution)/shard_map/ppermute | solution.py:38
  113.4 14.4 %collective-permute-start.18 = (bf16[128,2048]{1,0:T(8,128)(2,1)S(1)}, bf16[128,2048]{1,0:T(8,128)(2,1)S(1)}, u32[]{:S(2)}, u32[]{:S(2)}) collective-permute-start(bf16[128,2048]{1,0:T(8,128)(2,1)S(1)} %bitcast.27), channel_id=1, source_target_pairs={{0,32},{32,64},{64,96},{96,0},{1,33},{33,65},{65,97},{97,1},{2,34}... | collective-permute-start | bytes 1572872 | tf_op jit(solution)/shard_map/ppermute | solution.py:38
  117.6 13.7 %all-to-all-start.1 = ((bf16[16,64,128]{2,1,0:T(8,128)(2,1)}), bf16[16,64,128]{2,1,0:T(8,128)(2,1)S(1)}, u32[]{:S(2)}, u32[]{:S(2)}) async-start(bf16[16,64,128]{2,1,0:T(8,128)(2,1)} %maximum_select_fusion), calls=%async_computation.1 | async-start | bytes 524288 | tf_op jit(solution)/shard_map/all_to_all | solution.py:47
  122.5 16.0 %collective-permute-start.20 = (bf16[128,2048]{1,0:T(8,128)(2,1)S(1)}, bf16[128,2048]{1,0:T(8,128)(2,1)S(1)}, u32[]{:S(2)}, u32[]{:S(2)}) collective-permute-start(bf16[128,2048]{1,0:T(8,128)(2,1)S(1)} %bitcast.31), channel_id=1, source_target_pairs={{0,32},{32,64},{64,96},{96,0},{1,33},{33,65},{65,97},{97,1},{2,34}... | collective-permute-start | bytes 1572872 | tf_op jit(solution)/shard_map/ppermute | solution.py:38
  122.9 15.6 %collective-permute-start.21 = (bf16[128,2048]{1,0:T(8,128)(2,1)S(1)}, bf16[128,2048]{1,0:T(8,128)(2,1)S(1)}, u32[]{:S(2)}, u32[]{:S(2)}) collective-permute-start(bf16[128,2048]{1,0:T(8,128)(2,1)S(1)} %bitcast.28), channel_id=1, source_target_pairs={{0,96},{32,0},{64,32},{96,64},{1,97},{33,1},{65,33},{97,65},{2,98}... | collective-permute-start | bytes 1572872 | tf_op jit(solution)/shard_map/ppermute | solution.py:38
  125.9 22.4 %collective-permute-start.17 = (bf16[128,2048]{1,0:T(8,128)(2,1)S(1)}, bf16[128,2048]{1,0:T(8,128)(2,1)}, u32[]{:S(2)}, u32[]{:S(2)}) collective-permute-start(bf16[128,2048]{1,0:T(8,128)(2,1)S(1)} %collective-permute-done.16.k1), channel_id=1, source_target_pairs={{0,96},{32,0},{64,32},{96,64},{1,97},{33,1},{65,33},{97,65},{2,98}... | collective-permute-start | bytes 1572872 | tf_op jit(solution)/shard_map/ppermute | solution.py:38
  127.8 21.3 %collective-permute-start.19 = (bf16[128,2048]{1,0:T(8,128)(2,1)S(1)}, bf16[128,2048]{1,0:T(8,128)(2,1)}, u32[]{:S(2)}, u32[]{:S(2)}) collective-permute-start(bf16[128,2048]{1,0:T(8,128)(2,1)S(1)} %collective-permute-done.18.v3), channel_id=1, source_target_pairs={{0,32},{32,64},{64,96},{96,0},{1,33},{33,65},{65,97},{97,1},{2,34}... | collective-permute-start | bytes 1572872 | tf_op jit(solution)/shard_map/ppermute | solution.py:38
  (21 other events, 181.1 us)

commit v2 on v1

--- a/solution.py
+++ b/solution.py
@@ -47,7 +47,7 @@
     return lax.all_to_all(array, "mem", 0, 0, axis_index_groups=groups)
 
 
-def prepare_kernel(place, lists, queries, grads, keys, values, q, g, kv, sems):
+def prepare_kernel(place, queries, grads, keys, values, q, g, kv, sems):
     z, c, k = place[0], place[1], place[2]
     cols = pl.ds(pl.multiple_of(c * DH, DH), DH)
     pairs = []
@@ -63,28 +63,27 @@
     copies = [pltpu.make_async_copy(a, b, sems.at[n]) for n, (a, b) in enumerate(pairs)]
     for copy in copies:
         copy.start()
-    q[QPER, :TOPB, :TOPB] = lists[...].astype(F32).astype(BF)
     for copy in copies:
         copy.wait()
 
 
-def prepare(place, queries, grads, keys, values, lists):
+def prepare(place, queries, grads, keys, values):
     smem = pl.BlockSpec(memory_space=pltpu.SMEM)
     vmem = pl.BlockSpec(memory_space=pltpu.VMEM)
-    hbm = pl.BlockSpec(memory_space=pltpu.HBM)
+    far = pl.BlockSpec(memory_space=pl.ANY)
     return pl.pallas_call(
         prepare_kernel,
         out_shape=(
-            jax.ShapeDtypeStruct((QPER + 1, BLK, DH), BF),
+            jax.ShapeDtypeStruct((QPER, BLK, DH), BF),
             jax.ShapeDtypeStruct((QPER, BLK, DH), BF),
             jax.ShapeDtypeStruct((H, 2 * BLK, DH), BF),
         ),
-        in_specs=[smem, vmem] + [hbm] * 4,
+        in_specs=[smem] + [far] * 4,
         out_specs=(vmem, vmem, vmem),
         scratch_shapes=[pltpu.SemaphoreType.DMA((2 * QPER + 2 * H,))],
         compiler_params=pltpu.CompilerParams(vmem_limit_bytes=60 * MB),
         name="prepare",
-    )(place, lists, queries, grads, keys, values)
+    )(place, queries, grads, keys, values)
 
 
 def list_kernel(place, l0, l1, l2, l3, home, ents):
@@ -123,13 +122,14 @@
         out_shape=jax.ShapeDtypeStruct((COUNT + 8,), jnp.int32),
         in_specs=[smem] * 6,
         out_specs=smem,
+        compiler_params=pltpu.CompilerParams(vmem_limit_bytes=MB),
         name="entry_list",
     )(place, *lists, home)
 
 
 def fetch(qrefs, grefs, kvrefs, qs, gs, kv, sems):
     pairs = [(ref, kv.at[p]) for p, ref in enumerate(kvrefs)]
-    pairs += [(ref.at[:QPER], qs.at[r]) for r, ref in enumerate(qrefs)]
+    pairs += [(ref, qs.at[r]) for r, ref in enumerate(qrefs)]
     pairs += [(ref, gs.at[r]) for r, ref in enumerate(grefs)]
     copies = [pltpu.make_async_copy(a, b, sems.at[n]) for n, (a, b) in enumerate(pairs)]
     for copy in copies:
@@ -342,7 +342,7 @@
         in_specs=[smem] + [vmem] * 6,
         out_specs=(far, far),
         scratch_shapes=[pltpu.SemaphoreType.DMA((6,))],
-        compiler_params=pltpu.CompilerParams(vmem_limit_bytes=16 * MB),
+        compiler_params=pltpu.CompilerParams(vmem_limit_bytes=8 * MB),
         name="place_near",
     )(place, *kparts, *vparts)
 
@@ -359,7 +359,7 @@
         out_specs=(far, far),
         scratch_shapes=[pltpu.SemaphoreType.DMA((2,))],
         input_output_aliases={3: 0, 4: 1},
-        compiler_params=pltpu.CompilerParams(vmem_limit_bytes=16 * MB),
+        compiler_params=pltpu.CompilerParams(vmem_limit_bytes=8 * MB),
         name="place_far",
     )(place, k_far, v_far, *near)
 
@@ -378,21 +378,20 @@
     c, k = m // 2, m % 2
     place = jnp.stack([z, c, k]).astype(jnp.int32)
 
-    q_own, g_own, kv_cat = prepare(place, queries, grad_out, mem_keys, mem_values, block_lists)
-    kv_cat, l_far = lax.optimization_barrier((kv_cat, over_z(block_lists, 2)))
+    q_own, g_own, kv_cat = prepare(place, queries, grad_out, mem_keys, mem_values)
+    lists = tuple(over_z(block_lists, shift) for shift in (-1, 2, 1))
+    kv_cat, lists = lax.optimization_barrier((kv_cat, lists))
+    ents = make_list(place, (block_lists,) + lists, block_home)
     q_prev = over_z(q_own, 1)
     g_next = over_z(g_own, -1)
     g_prev = over_z(g_own, 1)
     q_next = over_z(q_own, -1)
-    kv_own, q_prev, g_next, g_prev, q_next = lax.optimization_barrier(
-        (plane_exchange(kv_cat), q_prev, g_next, g_prev, q_next)
+    kv_own, q_prev, g_next, g_prev, q_next, ents = lax.optimization_barrier(
+        (plane_exchange(kv_cat), q_prev, g_next, g_prev, q_next, ents)
     )
     q_far = over_z(q_prev, 1)
     g_far = over_z(g_next, -1)
     kvs = (kv_own, swap_cores(kv_own))
-    l_prev = q_prev[QPER, :TOPB, :TOPB].astype(jnp.int32)
-    l_next = q_next[QPER, :TOPB, :TOPB].astype(jnp.int32)
-    ents = make_list(place, (block_lists, l_next, l_far, l_prev), block_home)
     xparts = (q_own, q_next, q_far, q_prev, g_own, g_next, g_far, g_prev)
 
     stat = forward(ents, xparts, kvs)
@@ -406,11 +405,6 @@
     v_next = over_z(v_own, -1)
     k_next = over_z(k_own, -1)
     k_prev = over_z(k_own, 1)
-    v_far = over_z(v_prev, 1)
-    k_far = over_z(k_next, -1)
-    near = place_near(place, (k_own, k_next, k_prev), (v_own, v_next, v_prev))
-    grad_keys, grad_values = place_far(place, near, k_far, v_far)
-
     dq_sum = (
         dq0
         + over_z(dq1, 1).astype(F32)
@@ -424,6 +418,11 @@
     whole = jnp.where(
         k == 0, jnp.concatenate([keep, got], axis=0), jnp.concatenate([got, keep], axis=0)
     )
+    whole, v_prev, k_next = lax.optimization_barrier((whole, v_prev, k_next))
+    v_far = over_z(v_prev, 1)
+    k_far = over_z(k_next, -1)
+    near = place_near(place, (k_own, k_next, k_prev), (v_own, v_next, v_prev))
+    grad_keys, grad_values = place_far(place, near, k_far, v_far)
     grad_queries = rows_first(plane_exchange(whole))
     return grad_queries, grad_keys, grad_values
 

time: 154 us -> 144 us (0.935); the launches traced: 151 us -> 144 us
  local copies, waits for them, and re-layouts: 8.03 us -> 2.55 us
  Pallas kernels: 39.5 us -> 36.9 us
  waiting for transfers between devices: 51.4 us -> 49.4 us
  starting transfers between devices: 48 us -> 49.9 us
    ppermute x19 -> x21, waiting for transfers between devices: 40.8 us -> 31.6 us  [over_z(): return lax.ppermute(array, 'dp', [(i, (i + shift) % NZ) for i in range(NZ)])]
    all_to_all x3, waiting for transfers between devices: 6.69 us -> 13.9 us  [plane_exchange(): return lax.all_to_all(array, 'mem', 0, 0, axis_index_groups=groups)]
    unnamed x41 -> x19, local copies, waits for them, and re-layouts: 7.01 us -> 1.54 us
    ppermute x19 -> x21, starting transfers between devices: 29.1 us -> 33.3 us  [over_z(): return lax.ppermute(array, 'dp', [(i, (i + shift) % NZ) for i in range(NZ)])]
    all_to_all x3, starting transfers between devices: 18.9 us -> 16.5 us  [plane_exchange(): return lax.all_to_all(array, 'mem', 0, 0, axis_index_groups=groups)]
  transfers between devices with their start and end apart: 25 -> 27, of which waited for: 15 -> 13; matrix products, arithmetic and copies ran while one was open for 2% -> 3% of each run, Pallas kernels for 7% -> 8%
where the time goes in v2:
time: 144 us
  starting transfers between devices  49.9 us (35%)
  waiting for transfers between devices  49.4 us (34%)
  Pallas kernels  36.9 us (26%)
  other arithmetic  3.84 us (3%)
  local copies, waits for them, and re-layouts  2.55 us (2%)
    ppermute x21, starting transfers between devices, over_z(): return lax.ppermute(array, 'dp', [(i, (i + shift) % NZ) for i in range(NZ)])  33.3 us
    ppermute x21, waiting for transfers between devices, over_z(): return lax.ppermute(array, 'dp', [(i, (i + shift) % NZ) for i in range(NZ)])  31.6 us
    all_to_all x3, starting transfers between devices, plane_exchange(): return lax.all_to_all(array, 'mem', 0, 0, axis_index_groups=groups)  16.5 us
    pallas_call x1, Pallas kernels, backward(): pl.pallas_call(bwd_kernel, out_shape=tuple(outs), in_specs=[smem] + [vmem...  14.3 us
    all_to_all x3, waiting for transfers between devices, plane_exchange(): return lax.all_to_all(array, 'mem', 0, 0, axis_index_groups=groups)  13.9 us
    pallas_call x1, Pallas kernels, forward(): pl.pallas_call(fwd_kernel, out_shape=jax.ShapeDtypeStruct((3, NQ, DH), F3...  9.57 us
    pallas_call x1, Pallas kernels, make_list(): pl.pallas_call(list_kernel, out_shape=jax.ShapeDtypeStruct((COUNT + 8,),...  4.94 us
    ppermute x3, waiting for transfers between devices, swap_cores(): return lax.ppermute(array, 'mem', [(i, i ^ 1) for i in range(2 * NCHIP)])  3.99 us
  transfers between devices with their start and end apart: 27, of which 13 were waited for; matrix products, arithmetic and copies ran while one was open for 3% of the time, Pallas kernels for 8%

profile of v2, /device:TPU:0, one launch (start us, length us, event | category | flops | bytes accessed | tf_op | source)
XLA Modules:
  0.0 143.5 jit_solution(15867361571565992839)
XLA Ops:
  0.6 4.0 %collective-permute-start.1 = (s32[16,16]{1,0:T(8,128)}, s32[16,16]{1,0:T(8,128)S(1)}, u32[]{:S(2)}, u32[]{:S(2)}) collective-permute-start(s32[16,16]{1,0:T(8,128)} %l0.1), channel_id=1, source_target_pairs={{0,64},{32,96},{64,0},{96,32},{1,65},{33,97},{65,1},{97,33},{2,66}... | collective-permute-start | bytes 3080 | tf_op jit(solution)/shard_map/ppermute | solution.py:38
  7.3 3.6 %prepare.1 = (bf16[8,128,128]{2,1,0:T(8,128)(2,1)}, bf16[8,128,128]{2,1,0:T(8,128)(2,1)}, bf16[16,256,128]{2,1,0:T(8,128)(2,1)}) custom-call(s32[3]{0:T(128)} %pad_add_fusion.place, bf16[2048,2048]{1,0:T(8,128)(2,1)} %queries.1, bf16[2048,2048]{1,0:T(8,128)(2,1)} %grads.1, bf16[512,2048]{1,0:T(8,128)(2,1)} %keys.1, bf16[512,2048]{1,0:T(8,128)(2,1)} %values.1), custom_call_target="tpu_custom_call" | custom-call | tf_op jit(solution)/shard_map/prepare/pallas_call | solution.py:74
  11.0 7.2 %all-to-all-start = ((bf16[16,256,128]{2,1,0:T(8,128)(2,1)}), bf16[16,256,128]{2,1,0:T(8,128)(2,1)S(1)}, u32[]{:S(2)}, u32[]{:S(2)}) async-start(bf16[16,256,128]{2,1,0:T(8,128)(2,1)} %get-tuple-element.30), calls=%async_computation | async-start | bytes 2097152 | tf_op jit(solution)/shard_map/all_to_all | solution.py:47
  21.3 2.2 %collective-permute-start.4 = (bf16[8,128,128]{2,1,0:T(8,128)(2,1)S(1)}, bf16[8,128,128]{2,1,0:T(8,128)(2,1)S(1)}, u32[]{:S(2)}, u32[]{:S(2)}) collective-permute-start(bf16[8,128,128]{2,1,0:T(8,128)(2,1)S(1)} %copy-done.1), channel_id=1, source_target_pairs={{0,96},{32,0},{64,32},{96,64},{1,97},{33,1},{65,33},{97,65},{2,98}... | collective-permute-start | bytes 786440 | tf_op jit(solution)/shard_map/ppermute | solution.py:38
  23.5 4.9 %entry_list.1.ents = s32[528]{0:T(1024)S(1)} custom-call(s32[3]{0:T(128)S(1)} %copy-done.2, s32[16,16]{1,0:T(8,128)S(1)} %copy-done.3, s32[16,16]{1,0:T(8,128)S(1)} %collective-permute-done.l1, s32[16,16]{1,0:T(8,128)S(1)} %collective-permute-done.1.l2, s32[16,16]{1,0:T(8,128)S(1)} %collective-permute-done.2.l3, s32[128]{0:T(128)S(1)} %copy-done.4), custom_call_target="tpu_custom_call" | custom-call | tf_op jit(solution)/shard_map/entry_list/pallas_call | solution.py:120
  28.5 2.1 %collective-permute-done.3.q3 = bf16[8,128,128]{2,1,0:T(8,128)(2,1)S(1)} collective-permute-done((bf16[8,128,128]{2,1,0:T(8,128)(2,1)S(1)}, bf16[8,128,128]{2,1,0:T(8,128)(2,1)S(1)}, u32[]{:S(2)}, u32[]{:S(2)}) %collective-permute-start.3) | collective-permute-done | bytes 262176 | tf_op jit(solution)/shard_map/ppermute | solution.py:38
  30.6 3.0 %collective-permute-done.5.g3 = bf16[8,128,128]{2,1,0:T(8,128)(2,1)S(1)} collective-permute-done((bf16[8,128,128]{2,1,0:T(8,128)(2,1)S(1)}, bf16[8,128,128]{2,1,0:T(8,128)(2,1)S(1)}, u32[]{:S(2)}, u32[]{:S(2)}) %collective-permute-start.5) | collective-permute-done | bytes 262176 | tf_op jit(solution)/shard_map/ppermute | solution.py:38
  35.5 2.2 %collective-permute-start.8 = (bf16[8,128,128]{2,1,0:T(8,128)(2,1)S(1)}, bf16[8,128,128]{2,1,0:T(8,128)(2,1)S(1)}, u32[]{:S(2)}, u32[]{:S(2)}) collective-permute-start(bf16[8,128,128]{2,1,0:T(8,128)(2,1)S(1)} %collective-permute-done.4.g1), channel_id=1, source_target_pairs={{0,96},{32,0},{64,32},{96,64},{1,97},{33,1},{65,33},{97,65},{2,98}... | collective-permute-start | bytes 786440 | tf_op jit(solution)/shard_map/ppermute | solution.py:38
  37.8 6.7 %collective-permute-done.7.q2 = bf16[8,128,128]{2,1,0:T(8,128)(2,1)S(1)} collective-permute-done((bf16[8,128,128]{2,1,0:T(8,128)(2,1)S(1)}, bf16[8,128,128]{2,1,0:T(8,128)(2,1)S(1)}, u32[]{:S(2)}, u32[]{:S(2)}) %collective-permute-start.7) | collective-permute-done | bytes 262176 | tf_op jit(solution)/shard_map/ppermute | solution.py:38
  44.5 9.6 %forward.1.s0 = f32[3,32,128]{2,1,0:T(8,128)S(1)} custom-call(s32[528]{0:T(1024)S(1)} %entry_list.1.ents, bf16[8,128,128]{2,1,0:T(8,128)(2,1)S(1)} %copy-done, bf16[8,128,128]{2,1,0:T(8,128)(2,1)S(1)} %collective-permute-done.6.q1, bf16[8,128,128]{2,1,0:T(8,128)(2,1)S(1)} %collective-permute-done.7.q2, bf16[8,128,128]{2,1,0:T(8,128)(2,1)S(1)} %collective-permute-done.3.q3, ...), custom_call_target="tpu_custom_call" | custom-call | tf_op jit(solution)/shard_map/forward/pallas_call | solution.py:194
  58.9 2.5 %collective-permute-done.11.s2 = f32[3,32,128]{2,1,0:T(8,128)S(1)} collective-permute-done((f32[3,32,128]{2,1,0:T(8,128)S(1)}, f32[3,32,128]{2,1,0:T(8,128)S(1)}, u32[]{:S(2)}, u32[]{:S(2)}) %collective-permute-start.11) | collective-permute-done | bytes 49184 | tf_op jit(solution)/shard_map/ppermute | solution.py:38
  62.9 14.3 %backward.1 = (f32[8,128,128]{2,1,0:T(8,128)S(1)}, bf16[8,128,128]{2,1,0:T(8,128)(2,1)S(1)}, bf16[8,128,128]{2,1,0:T(8,128)(2,1)S(1)}, bf16[8,128,128]{2,1,0:T(8...) custom-call(s32[528]{0:T(1024)S(1)} %entry_list.1.ents, f32[3,32,128]{2,1,0:T(8,128)S(1)} %forward.1.s0, ...), custom_call_target="tpu_custom_call" | custom-call | tf_op jit(solution)/shard_map/backward/pallas_call | solution.py:292
  78.6 2.7 %collective-permute-done.17 = bf16[16,256,128]{2,1,0:T(8,128)(2,1)S(1)} collective-permute-done((bf16[16,256,128]{2,1,0:T(8,128)(2,1)S(1)}, bf16[16,256,128]{2,1,0:T(8,128)(2,1)S(1)}, u32[]{:S(2)}, u32[]{:S(2)}) %collective-permute-start.17) | collective-permute-done | bytes 1048608 | tf_op jit(solution)/shard_map/ppermute | solution.py:42
  82.6 5.8 %all-to-all-start.1 = ((bf16[16,256,128]{2,1,0:T(8,128)(2,1)}), bf16[16,256,128]{2,1,0:T(8,128)(2,1)S(1)}, u32[]{:S(2)}, u32[]{:S(2)}) async-start(bf16[16,256,128]{2,1,0:T(8,128)(2,1)} %add_convert_fusion), calls=%async_computation.1 | async-start | bytes 2097152 | tf_op jit(solution)/shard_map/all_to_all | solution.py:47
  88.5 3.2 %collective-permute-start.14 = (bf16[8,128,128]{2,1,0:T(8,128)(2,1)S(1)}, bf16[8,128,128]{2,1,0:T(8,128)(2,1)}, u32[]{:S(2)}, u32[]{:S(2)}) collective-permute-start(bf16[8,128,128]{2,1,0:T(8,128)(2,1)S(1)} %copy-done.6), channel_id=1, source_target_pairs={{0,96},{32,0},{64,32},{96,64},{1,97},{33,1},{65,33},{97,65},{2,98}... | collective-permute-start | bytes 786440 | tf_op jit(solution)/shard_map/ppermute | solution.py:38
  93.5 13.0 %all-to-all-done.1 = bf16[16,256,128]{2,1,0:T(8,128)(2,1)S(1)} async-done(((bf16[16,256,128]{2,1,0:T(8,128)(2,1)}), bf16[16,256,128]{2,1,0:T(8,128)(2,1)S(1)}, u32[]{:S(2)}, u32[]{:S(2)}) %all-to-all-start.1) | async-done | bytes 1048608 | tf_op jit(solution)/shard_map/all_to_all | solution.py:47
  106.9 3.2 %collective-permute-start.19 = (bf16[128,2048]{1,0:T(8,128)(2,1)S(1)}, bf16[128,2048]{1,0:T(8,128)(2,1)S(1)}, u32[]{:S(2)}, u32[]{:S(2)}) collective-permute-start(bf16[128,2048]{1,0:T(8,128)(2,1)S(1)} %bitcast.21), channel_id=1, source_target_pairs={{0,96},{32,0},{64,32},{96,64},{1,97},{33,1},{65,33},{97,65},{2,98}... | collective-permute-start | bytes 1572872 | tf_op jit(solution)/shard_map/ppermute | solution.py:38
  115.7 7.3 %collective-permute-done.18.v3 = bf16[128,2048]{1,0:T(8,128)(2,1)S(1)} collective-permute-done((bf16[128,2048]{1,0:T(8,128)(2,1)S(1)}, bf16[128,2048]{1,0:T(8,128)(2,1)S(1)}, u32[]{:S(2)}, u32[]{:S(2)}) %collective-permute-start.18) | collective-permute-done | bytes 524320 | tf_op jit(solution)/shard_map/ppermute | solution.py:38
  123.0 3.5 %all-to-all-start.2 = ((bf16[16,64,128]{2,1,0:T(8,128)(2,1)}), bf16[16,64,128]{2,1,0:T(8,128)(2,1)S(1)}, u32[]{:S(2)}, u32[]{:S(2)}) async-start(bf16[16,64,128]{2,1,0:T(8,128)(2,1)} %maximum_select_fusion), calls=%async_computation.2 | async-start | bytes 524288 | tf_op jit(solution)/shard_map/all_to_all | solution.py:47
  126.6 3.3 %collective-permute-start.20 = (bf16[128,2048]{1,0:T(8,128)(2,1)S(1)}, bf16[128,2048]{1,0:T(8,128)(2,1)}, u32[]{:S(2)}, u32[]{:S(2)}) collective-permute-start(bf16[128,2048]{1,0:T(8,128)(2,1)S(1)} %collective-permute-done.19.k1), channel_id=1, source_target_pairs={{0,96},{32,0},{64,32},{96,64},{1,97},{33,1},{65,33},{97,65},{2,98}... | collective-permute-start | bytes 1572872 | tf_op jit(solution)/shard_map/ppermute | solution.py:38
  129.9 4.1 %collective-permute-done.23.v1 = bf16[128,2048]{1,0:T(8,128)(2,1)S(1)} collective-permute-done((bf16[128,2048]{1,0:T(8,128)(2,1)S(1)}, bf16[128,2048]{1,0:T(8,128)(2,1)S(1)}, u32[]{:S(2)}, u32[]{:S(2)}) %collective-permute-start.23) | collective-permute-done | bytes 524320 | tf_op jit(solution)/shard_map/ppermute | solution.py:38
  134.0 2.3 %place_near.1 = (bf16[512,2048]{1,0:T(8,128)(2,1)}, bf16[512,2048]{1,0:T(8,128)(2,1)}) custom-call(s32[3]{0:T(128)S(1)} %copy-done.2, bf16[128,2048]{1,0:T(8,128)(2,1)S(1)} %bitcast.23, bf16[128,2048]{1,0:T(8,128)(2,1)S(1)} %collective-permute-done.19.k1, bf16[128,2048]{1,0:T(8,128)(2,1)S(1)} %collective-permute-done.22.k3, bf16[128,2048]{1,0:T(8,128)(2,1)S(1)} %bitcast.26, ...), custom_call_target="tpu_custom_call" | custom-call | tf_op jit(solution)/shard_map/place_near/pallas_call | solution.py:339
  137.0 4.1 %collective-permute-done.20.k2 = bf16[128,2048]{1,0:T(8,128)(2,1)} collective-permute-done((bf16[128,2048]{1,0:T(8,128)(2,1)S(1)}, bf16[128,2048]{1,0:T(8,128)(2,1)}, u32[]{:S(2)}, u32[]{:S(2)}) %collective-permute-start.20) | collective-permute-done | bytes 524320 | tf_op jit(solution)/shard_map/ppermute | solution.py:38
  141.3 2.2 %place_far.1 = (bf16[512,2048]{1,0:T(8,128)(2,1)}, bf16[512,2048]{1,0:T(8,128)(2,1)}) custom-call(s32[3]{0:T(128)S(1)} %copy-done.2, bf16[128,2048]{1,0:T(8,128)(2,1)} %collective-permute-done.20.k2, bf16[128,2048]{1,0:T(8,128)(2,1)} %collective-permute-done.21.v2, ...), custom_call_target="tpu_custom_call", output_to_operand_aliasing={{0}: (3, {}), {1}: (4, {})} | custom-call | tf_op jit(solution)/shard_map/place_far/pallas_call | solution.py:355
  (63 shorter events, 25.5 us)
Async XLA Ops:
  0.6 10.3 %collective-permute-start.1 = (s32[16,16]{1,0:T(8,128)}, s32[16,16]{1,0:T(8,128)S(1)}, u32[]{:S(2)}, u32[]{:S(2)}) collective-permute-start(s32[16,16]{1,0:T(8,128)} %l0.1), channel_id=1, source_target_pairs={{0,64},{32,96},{64,0},{96,32},{1,65},{33,97},{65,1},{97,33},{2,66}... | collective-permute-start | bytes 3080 | tf_op jit(solution)/shard_map/ppermute | solution.py:38
  4.7 6.3 %collective-permute-start = (s32[16,16]{1,0:T(8,128)}, s32[16,16]{1,0:T(8,128)S(1)}, u32[]{:S(2)}, u32[]{:S(2)}) collective-permute-start(s32[16,16]{1,0:T(8,128)} %l0.1), channel_id=1, source_target_pairs={{0,96},{32,0},{64,32},{96,64},{1,97},{33,1},{65,33},{97,65},{2,98}... | collective-permute-start | bytes 3080 | tf_op jit(solution)/shard_map/ppermute | solution.py:38
  5.4 5.6 %collective-permute-start.2 = (s32[16,16]{1,0:T(8,128)}, s32[16,16]{1,0:T(8,128)S(1)}, u32[]{:S(2)}, u32[]{:S(2)}) collective-permute-start(s32[16,16]{1,0:T(8,128)} %l0.1), channel_id=1, source_target_pairs={{0,32},{32,64},{64,96},{96,0},{1,33},{33,65},{65,97},{97,1},{2,34}... | collective-permute-start | bytes 3080 | tf_op jit(solution)/shard_map/ppermute | solution.py:38
  11.0 23.5 %all-to-all-start = ((bf16[16,256,128]{2,1,0:T(8,128)(2,1)}), bf16[16,256,128]{2,1,0:T(8,128)(2,1)S(1)}, u32[]{:S(2)}, u32[]{:S(2)}) async-start(bf16[16,256,128]{2,1,0:T(8,128)(2,1)} %get-tuple-element.30), calls=%async_computation | async-start | bytes 2097152 | tf_op jit(solution)/shard_map/all_to_all | solution.py:47
  18.2 10.3 %collective-permute-start.6 = (bf16[8,128,128]{2,1,0:T(8,128)(2,1)S(1)}, bf16[8,128,128]{2,1,0:T(8,128)(2,1)S(1)}, u32[]{:S(2)}, u32[]{:S(2)}) collective-permute-start(bf16[8,128,128]{2,1,0:T(8,128)(2,1)S(1)} %copy-done), channel_id=1, source_target_pairs={{0,96},{32,0},{64,32},{96,64},{1,97},{33,1},{65,33},{97,65},{2,98}... | collective-permute-start | bytes 786440 | tf_op jit(solution)/shard_map/ppermute | solution.py:38
  20.2 10.5 %collective-permute-start.3 = (bf16[8,128,128]{2,1,0:T(8,128)(2,1)S(1)}, bf16[8,128,128]{2,1,0:T(8,128)(2,1)S(1)}, u32[]{:S(2)}, u32[]{:S(2)}) collective-permute-start(bf16[8,128,128]{2,1,0:T(8,128)(2,1)S(1)} %copy-done), channel_id=1, source_target_pairs={{0,32},{32,64},{64,96},{96,0},{1,33},{33,65},{65,97},{97,1},{2,34}... | collective-permute-start | bytes 786440 | tf_op jit(solution)/shard_map/ppermute | solution.py:38
  20.3 13.4 %collective-permute-start.5 = (bf16[8,128,128]{2,1,0:T(8,128)(2,1)S(1)}, bf16[8,128,128]{2,1,0:T(8,128)(2,1)S(1)}, u32[]{:S(2)}, u32[]{:S(2)}) collective-permute-start(bf16[8,128,128]{2,1,0:T(8,128)(2,1)S(1)} %copy-done.1), channel_id=1, source_target_pairs={{0,32},{32,64},{64,96},{96,0},{1,33},{33,65},{65,97},{97,1},{2,34}... | collective-permute-start | bytes 786440 | tf_op jit(solution)/shard_map/ppermute | solution.py:38
  21.3 12.4 %collective-permute-start.4 = (bf16[8,128,128]{2,1,0:T(8,128)(2,1)S(1)}, bf16[8,128,128]{2,1,0:T(8,128)(2,1)S(1)}, u32[]{:S(2)}, u32[]{:S(2)}) collective-permute-start(bf16[8,128,128]{2,1,0:T(8,128)(2,1)S(1)} %copy-done.1), channel_id=1, source_target_pairs={{0,96},{32,0},{64,32},{96,64},{1,97},{33,1},{65,33},{97,65},{2,98}... | collective-permute-start | bytes 786440 | tf_op jit(solution)/shard_map/ppermute | solution.py:38
  34.5 9.9 %collective-permute-start.9 = (bf16[16,256,128]{2,1,0:T(8,128)(2,1)S(1)}, bf16[16,256,128]{2,1,0:T(8,128)(2,1)S(1)}, u32[]{:S(2)}, u32[]{:S(2)}) collective-permute-start(bf16[16,256,128]{2,1,0:T(8,128)(2,1)S(1)} %all-to-all-done.kva), channel_id=1, source_target_pairs={{0,1},{1,0},{2,3},{3,2},{4,5},{5,4},{6,7},{7,6},{8,9},{9,8},{10,11... | collective-permute-start | bytes 3145736 | tf_op jit(solution)/shard_map/ppermute | solution.py:42
  34.5 9.9 %collective-permute-start.7 = (bf16[8,128,128]{2,1,0:T(8,128)(2,1)S(1)}, bf16[8,128,128]{2,1,0:T(8,128)(2,1)S(1)}, u32[]{:S(2)}, u32[]{:S(2)}) collective-permute-start(bf16[8,128,128]{2,1,0:T(8,128)(2,1)S(1)} %collective-permute-done.3.q3), channel_id=1, source_target_pairs={{0,32},{32,64},{64,96},{96,0},{1,33},{33,65},{65,97},{97,1},{2,34}... | collective-permute-start | bytes 786440 | tf_op jit(solution)/shard_map/ppermute | solution.py:38
  35.5 8.9 %collective-permute-start.8 = (bf16[8,128,128]{2,1,0:T(8,128)(2,1)S(1)}, bf16[8,128,128]{2,1,0:T(8,128)(2,1)S(1)}, u32[]{:S(2)}, u32[]{:S(2)}) collective-permute-start(bf16[8,128,128]{2,1,0:T(8,128)(2,1)S(1)} %collective-permute-done.4.g1), channel_id=1, source_target_pairs={{0,96},{32,0},{64,32},{96,64},{1,97},{33,1},{65,33},{97,65},{2,98}... | collective-permute-start | bytes 786440 | tf_op jit(solution)/shard_map/ppermute | solution.py:38
  55.6 5.8 %collective-permute-start.11 = (f32[3,32,128]{2,1,0:T(8,128)S(1)}, f32[3,32,128]{2,1,0:T(8,128)S(1)}, u32[]{:S(2)}, u32[]{:S(2)}) collective-permute-start(f32[3,32,128]{2,1,0:T(8,128)S(1)} %forward.1.s0), channel_id=1, source_target_pairs={{0,64},{32,96},{64,0},{96,32},{1,65},{33,97},{65,1},{97,33},{2,66}... | collective-permute-start | bytes 147464 | tf_op jit(solution)/shard_map/ppermute | solution.py:38
  57.6 5.3 %collective-permute-start.10 = (f32[3,32,128]{2,1,0:T(8,128)S(1)}, f32[3,32,128]{2,1,0:T(8,128)S(1)}, u32[]{:S(2)}, u32[]{:S(2)}) collective-permute-start(f32[3,32,128]{2,1,0:T(8,128)S(1)} %forward.1.s0), channel_id=1, source_target_pairs={{0,32},{32,64},{64,96},{96,0},{1,33},{33,65},{65,97},{97,1},{2,34}... | collective-permute-start | bytes 147464 | tf_op jit(solution)/shard_map/ppermute | solution.py:38
  82.6 23.9 %all-to-all-start.1 = ((bf16[16,256,128]{2,1,0:T(8,128)(2,1)}), bf16[16,256,128]{2,1,0:T(8,128)(2,1)S(1)}, u32[]{:S(2)}, u32[]{:S(2)}) async-start(bf16[16,256,128]{2,1,0:T(8,128)(2,1)} %add_convert_fusion), calls=%async_computation.1 | async-start | bytes 2097152 | tf_op jit(solution)/shard_map/all_to_all | solution.py:47
  88.4 21.8 %collective-permute-start.13 = (bf16[8,128,128]{2,1,0:T(8,128)(2,1)S(1)}, bf16[8,128,128]{2,1,0:T(8,128)(2,1)}, u32[]{:S(2)}, u32[]{:S(2)}) collective-permute-start(bf16[8,128,128]{2,1,0:T(8,128)(2,1)S(1)} %copy-done.8), channel_id=1, source_target_pairs={{0,32},{32,64},{64,96},{96,0},{1,33},{33,65},{65,97},{97,1},{2,34}... | collective-permute-start | bytes 786440 | tf_op jit(solution)/shard_map/ppermute | solution.py:38
  88.5 21.7 %collective-permute-start.14 = (bf16[8,128,128]{2,1,0:T(8,128)(2,1)S(1)}, bf16[8,128,128]{2,1,0:T(8,128)(2,1)}, u32[]{:S(2)}, u32[]{:S(2)}) collective-permute-start(bf16[8,128,128]{2,1,0:T(8,128)(2,1)S(1)} %copy-done.6), channel_id=1, source_target_pairs={{0,96},{32,0},{64,32},{96,64},{1,97},{33,1},{65,33},{97,65},{2,98}... | collective-permute-start | bytes 786440 | tf_op jit(solution)/shard_map/ppermute | solution.py:38
  91.7 18.5 %collective-permute-start.15 = (bf16[8,128,128]{2,1,0:T(8,128)(2,1)S(1)}, bf16[8,128,128]{2,1,0:T(8,128)(2,1)}, u32[]{:S(2)}, u32[]{:S(2)}) collective-permute-start(bf16[8,128,128]{2,1,0:T(8,128)(2,1)S(1)} %get-tuple-element.45), channel_id=1, source_target_pairs={{0,64},{32,96},{64,0},{96,32},{1,65},{33,97},{65,1},{97,33},{2,66}... | collective-permute-start | bytes 786440 | tf_op jit(solution)/shard_map/ppermute | solution.py:38
  106.9 16.1 %collective-permute-start.18 = (bf16[128,2048]{1,0:T(8,128)(2,1)S(1)}, bf16[128,2048]{1,0:T(8,128)(2,1)S(1)}, u32[]{:S(2)}, u32[]{:S(2)}) collective-permute-start(bf16[128,2048]{1,0:T(8,128)(2,1)S(1)} %bitcast.24), channel_id=1, source_target_pairs={{0,32},{32,64},{64,96},{96,0},{1,33},{33,65},{65,97},{97,1},{2,34}... | collective-permute-start | bytes 1572872 | tf_op jit(solution)/shard_map/ppermute | solution.py:38
  106.9 16.1 %collective-permute-start.19 = (bf16[128,2048]{1,0:T(8,128)(2,1)S(1)}, bf16[128,2048]{1,0:T(8,128)(2,1)S(1)}, u32[]{:S(2)}, u32[]{:S(2)}) collective-permute-start(bf16[128,2048]{1,0:T(8,128)(2,1)S(1)} %bitcast.21), channel_id=1, source_target_pairs={{0,96},{32,0},{64,32},{96,64},{1,97},{33,1},{65,33},{97,65},{2,98}... | collective-permute-start | bytes 1572872 | tf_op jit(solution)/shard_map/ppermute | solution.py:38
  111.4 22.5 %collective-permute-start.23 = (bf16[128,2048]{1,0:T(8,128)(2,1)S(1)}, bf16[128,2048]{1,0:T(8,128)(2,1)S(1)}, u32[]{:S(2)}, u32[]{:S(2)}) collective-permute-start(bf16[128,2048]{1,0:T(8,128)(2,1)S(1)} %bitcast.25), channel_id=1, source_target_pairs={{0,96},{32,0},{64,32},{96,64},{1,97},{33,1},{65,33},{97,65},{2,98}... | collective-permute-start | bytes 1572872 | tf_op jit(solution)/shard_map/ppermute | solution.py:38
  111.9 22.1 %collective-permute-start.22 = (bf16[128,2048]{1,0:T(8,128)(2,1)S(1)}, bf16[128,2048]{1,0:T(8,128)(2,1)S(1)}, u32[]{:S(2)}, u32[]{:S(2)}) collective-permute-start(bf16[128,2048]{1,0:T(8,128)(2,1)S(1)} %bitcast.22), channel_id=1, source_target_pairs={{0,32},{32,64},{64,96},{96,0},{1,33},{33,65},{65,97},{97,1},{2,34}... | collective-permute-start | bytes 1572872 | tf_op jit(solution)/shard_map/ppermute | solution.py:38
  123.0 13.2 %all-to-all-start.2 = ((bf16[16,64,128]{2,1,0:T(8,128)(2,1)}), bf16[16,64,128]{2,1,0:T(8,128)(2,1)S(1)}, u32[]{:S(2)}, u32[]{:S(2)}) async-start(bf16[16,64,128]{2,1,0:T(8,128)(2,1)} %maximum_select_fusion), calls=%async_computation.2 | async-start | bytes 524288 | tf_op jit(solution)/shard_map/all_to_all | solution.py:47
  126.6 14.5 %collective-permute-start.20 = (bf16[128,2048]{1,0:T(8,128)(2,1)S(1)}, bf16[128,2048]{1,0:T(8,128)(2,1)}, u32[]{:S(2)}, u32[]{:S(2)}) collective-permute-start(bf16[128,2048]{1,0:T(8,128)(2,1)S(1)} %collective-permute-done.19.k1), channel_id=1, source_target_pairs={{0,96},{32,0},{64,32},{96,64},{1,97},{33,1},{65,33},{97,65},{2,98}... | collective-permute-start | bytes 1572872 | tf_op jit(solution)/shard_map/ppermute | solution.py:38
  129.9 11.4 %collective-permute-start.21 = (bf16[128,2048]{1,0:T(8,128)(2,1)S(1)}, bf16[128,2048]{1,0:T(8,128)(2,1)}, u32[]{:S(2)}, u32[]{:S(2)}) collective-permute-start(bf16[128,2048]{1,0:T(8,128)(2,1)S(1)} %collective-permute-done.18.v3), channel_id=1, source_target_pairs={{0,32},{32,64},{64,96},{96,0},{1,33},{33,65},{65,97},{97,1},{2,34}... | collective-permute-start | bytes 1572872 | tf_op jit(solution)/shard_map/ppermute | solution.py:38
  (12 other events, 76.5 us)

commit v3 on v2

--- a/solution.py
+++ b/solution.py
@@ -1,3 +1,5 @@
+import functools
+
 import jax
 import jax.numpy as jnp
 from jax import lax
@@ -15,7 +17,10 @@
 NQ = NZ * QPER
 NB = 2 * NCHIP
 NENT = NQ * TOPB
-COUNT = NENT + 8
+EARLY = (0, 1, 3)
+LATE = (2,)
+LATE_AT = len(EARLY) * QPER * TOPB + 8
+COUNT = LATE_AT + len(LATE) * QPER * TOPB + 8
 NCOPY = 2 * NZ + 2
 UNROLL_F = 8
 UNROLL_B = 8
@@ -107,12 +112,14 @@
 
         return lax.fori_loop(0, QPER, block, n)
 
-    n = jnp.int32(0)
-    for r, lists in enumerate((l0, l1, l2, l3)):
-        n = group(r, lists, n)
-    for u in range(8):
-        ents[n + u] = (NQ << 15) | (NENT << 5)
-    ents[COUNT] = n
+    every = (l0, l1, l2, l3)
+    for part, (start, groups) in enumerate(((0, EARLY), (LATE_AT, LATE))):
+        n = jnp.int32(start)
+        for r in groups:
+            n = group(r, every[r], n)
+        for u in range(8):
+            ents[n + u] = ((NQ + groups[0] * QPER) << 15) | (NENT << 5)
+        ents[COUNT + part] = n - start
 
 
 def make_list(place, lists, home):
@@ -127,10 +134,10 @@
     )(place, *lists, home)
 
 
-def fetch(qrefs, grefs, kvrefs, qs, gs, kv, sems):
+def fetch(groups, qrefs, grefs, kvrefs, qs, gs, kv, sems):
     pairs = [(ref, kv.at[p]) for p, ref in enumerate(kvrefs)]
-    pairs += [(ref, qs.at[r]) for r, ref in enumerate(qrefs)]
-    pairs += [(ref, gs.at[r]) for r, ref in enumerate(grefs)]
+    pairs += [(ref, qs.at[r]) for r, ref in zip(groups, qrefs)]
+    pairs += [(ref, gs.at[r]) for r, ref in zip(groups, grefs)]
     copies = [pltpu.make_async_copy(a, b, sems.at[n]) for n, (a, b) in enumerate(pairs)]
     for copy in copies:
         copy.start()
@@ -143,8 +150,12 @@
     return (q >> 3) & 3, q & 7, q, (p >> 5) & 1023, b >> 4, b & 15
 
 
-def fwd_kernel(ents, q0, q1, q2, q3, g0, g1, g2, g3, kva, kvb, out, qs, gs, kv, st, sems):
-    copies = fetch((q0, q1, q2, q3), (g0, g1, g2, g3), (kva, kvb), qs, gs, kv, sems)
+def fwd_kernel(groups, start, ents, before, *refs):
+    size = len(groups)
+    out, qs, gs, kv, st, sems = refs[2 * size + 2 :]
+    copies = fetch(
+        groups, refs[:size], refs[size : 2 * size], refs[2 * size : 2 * size + 2], qs, gs, kv, sems
+    )
     st[0] = jnp.full((NENT + 8, DH), -1e30, F32)
     st[1] = jnp.zeros((NENT + 8, DH), F32)
     st[2] = jnp.zeros((NENT + 8, DH), F32)
@@ -152,7 +163,7 @@
         copy.wait()
 
     def body(n, carry):
-        parts = [unpack(ents[UNROLL_F * n + u]) for u in range(UNROLL_F)]
+        parts = [unpack(ents[start + UNROLL_F * n + u]) for u in range(UNROLL_F)]
         scores = [dot(kv[p[4], p[5], :BLK], qs[p[0], p[1]], NT) * SCALE for p in parts]
         dprob = [dot(kv[p[4], p[5], BLK:], gs[p[0], p[1]], NT) for p in parts]
         highs = [jnp.max(x, axis=0, keepdims=True) for x in scores]
@@ -164,20 +175,24 @@
             st[2, row, :] = jnp.sum(e.astype(BF).astype(F32) * d, axis=0, keepdims=True)
         return carry
 
-    lax.fori_loop(0, (ents[COUNT] + UNROLL_F - 1) // UNROLL_F, body, 0)
-    high = st[0, 0:NQ]
-    for e in range(1, TOPB):
-        high = jnp.maximum(high, st[0, e * NQ : (e + 1) * NQ])
-    total = jnp.zeros((NQ, DH), F32)
-    prod = jnp.zeros((NQ, DH), F32)
-    for e in range(TOPB):
-        rows = slice(e * NQ, (e + 1) * NQ)
-        weight = jnp.exp(st[0, rows] - high)
-        total = total + weight * st[1, rows]
-        prod = prod + weight * st[2, rows]
-    out[0] = high
-    out[1] = total
-    out[2] = prod
+    part = 0 if start == 0 else 1
+    lax.fori_loop(0, (ents[COUNT + part] + UNROLL_F - 1) // UNROLL_F, body, 0)
+    out[...] = before[...]
+    for r in groups:
+        rows = [slice(e * NQ + r * QPER, e * NQ + (r + 1) * QPER) for e in range(TOPB)]
+        high = st[0, rows[0]]
+        for row in rows[1:]:
+            high = jnp.maximum(high, st[0, row])
+        total = jnp.zeros((QPER, DH), F32)
+        prod = jnp.zeros((QPER, DH), F32)
+        for row in rows:
+            weight = jnp.exp(st[0, row] - high)
+            total = total + weight * st[1, row]
+            prod = prod + weight * st[2, row]
+        at = slice(r * QPER, (r + 1) * QPER)
+        out[0, at] = high
+        out[1, at] = total
+        out[2, at] = prod
 
 
 def scratch_in():
@@ -188,19 +203,20 @@
     ]
 
 
-def forward(ents, xparts, kvs):
-    smem = pl.BlockSpec(memory_space=pltpu.SMEM)
+def forward(groups, start, ents, before, qparts, gparts, kvs):
+    smem = pl.BlockSpec(memory_space=pltpu.SMEM)
+    vmem = pl.BlockSpec(memory_space=pltpu.VMEM)
     far = pl.BlockSpec(memory_space=pl.ANY)
     return pl.pallas_call(
-        fwd_kernel,
+        functools.partial(fwd_kernel, groups, start),
         out_shape=jax.ShapeDtypeStruct((3, NQ, DH), F32),
-        in_specs=[smem] + [far] * 10,
-        out_specs=pl.BlockSpec(memory_space=pltpu.VMEM),
+        in_specs=[smem, vmem] + [far] * (2 * len(groups) + 2),
+        out_specs=vmem,
         scratch_shapes=scratch_in()
         + [pltpu.VMEM((3, NENT + 8, DH), F32), pltpu.SemaphoreType.DMA((NCOPY,))],
         compiler_params=pltpu.CompilerParams(vmem_limit_bytes=14 * MB),
         name="forward",
-    )(ents, *xparts, *kvs)
+    )(ents, before, *qparts, *gparts, *kvs)
 
 
 def bwd_kernel(
@@ -208,7 +224,7 @@
     dq0, dq1, dq2, dq3, own, other,
     qs, gs, kv, dq, dkv, away, dqs, lse, delta, sems, outsems,
 ):
-    copies = fetch((q0, q1, q2, q3), (g0, g1, g2, g3), (kva, kvb), qs, gs, kv, sems)
+    copies = fetch(range(NZ), (q0, q1, q2, q3), (g0, g1, g2, g3), (kva, kvb), qs, gs, kv, sems)
 
     def clear(i, carry):
         zero = jnp.zeros((BLK, DH), F32)
@@ -238,11 +254,15 @@
     for copy in copies:
         copy.wait()
 
-    lse[NQ : NQ + 8] = jnp.full((8, DH), 1e30, F32)
-    delta[NQ : NQ + 8] = jnp.zeros((8, DH), F32)
+    lse[NQ:] = jnp.full((NQ, DH), 1e30, F32)
+    delta[NQ:] = jnp.zeros((NQ, DH), F32)
+
+    early = (ents[COUNT] + UNROLL_B - 1) // UNROLL_B
+    late = (ents[COUNT + 1] + UNROLL_B - 1) // UNROLL_B
 
     def body(n, carry):
-        parts = [unpack(ents[UNROLL_B * n + u]) for u in range(UNROLL_B)]
+        at = jnp.where(n < early, n * UNROLL_B, LATE_AT + (n - early) * UNROLL_B)
+        parts = [unpack(ents[at + u]) for u in range(UNROLL_B)]
         keys = [kv[p[4], p[5], :BLK] for p in parts]
         quer = [qs[p[0], p[1]] for p in parts]
         grad = [gs[p[0], p[1]] for p in parts]
@@ -263,7 +283,7 @@
             dq[p[0] * QPER + p[1]] += c
         return carry
 
-    lax.fori_loop(0, (ents[COUNT] + UNROLL_B - 1) // UNROLL_B, body, 0)
+    lax.fori_loop(0, early + late, body, 0)
     away[...] = dkv[NCHIP:].astype(BF)
     sends = [pltpu.make_async_copy(away, other, outsems.at[0])]
     sends[0].start()
@@ -300,8 +320,8 @@
             pltpu.VMEM((NB, 2 * BLK, DH), F32),
             pltpu.VMEM(pair, BF),
             pltpu.VMEM((NQ - QPER,) + tile, BF),
-            pltpu.VMEM((NQ + 8, DH), F32),
-            pltpu.VMEM((NQ + 8, DH), F32),
+            pltpu.VMEM((2 * NQ, DH), F32),
+            pltpu.VMEM((2 * NQ, DH), F32),
             pltpu.SemaphoreType.DMA((NCOPY,)),
             pltpu.SemaphoreType.DMA((6,)),
         ],
@@ -394,7 +414,9 @@
     kvs = (kv_own, swap_cores(kv_own))
     xparts = (q_own, q_next, q_far, q_prev, g_own, g_next, g_far, g_prev)
 
-    stat = forward(ents, xparts, kvs)
+    stat = jnp.zeros((3, NQ, DH), F32)
+    stat = forward(EARLY, 0, ents, stat, (q_own, q_next, q_prev), (g_own, g_next, g_prev), kvs)
+    stat = forward(LATE, LATE_AT, ents, stat, (q_far,), (g_far,), kvs)
     stats = (stat, over_z(stat, 1), over_z(stat, 2), over_z(stat, -1))
     dq0, dq1, dq2, dq3, own, other = backward(ents, stats, xparts, kvs)
 

time: 144 us -> 139 us (0.965)
  waiting for transfers between devices: 49.4 us -> 45.4 us
  starting transfers between devices: 49.9 us -> 46.8 us
    ppermute x21, waiting for transfers between devices: 31.6 us -> 25.8 us  [over_z(): return lax.ppermute(array, 'dp', [(i, (i + shift) % NZ) for i in range(NZ)])]
    ppermute x21, starting transfers between devices: 33.3 us -> 29.7 us  [over_z(): return lax.ppermute(array, 'dp', [(i, (i + shift) % NZ) for i in range(NZ)])]
    all_to_all x3, waiting for transfers between devices: 13.9 us -> 15.6 us  [plane_exchange(): return lax.all_to_all(array, 'mem', 0, 0, axis_index_groups=groups)]
    pallas_call x1 -> x2, Pallas kernels: 9.57 us -> 10.4 us  [forward(): pl.pallas_call(functools.partial(fwd_kernel, groups, start), out_shape=ja...]
  transfers between devices with their start and end apart: 27 -> 27, of which waited for: 13 -> 13; matrix products, arithmetic and copies ran while one was open for 3% -> 3% of each run, Pallas kernels for 8% -> 13%
where the time goes in v3:
time: 139 us; the launch traced here: 137 us
  starting transfers between devices  46.8 us (34%)
  waiting for transfers between devices  45.4 us (33%)
  Pallas kernels  37.9 us (27%)
  other arithmetic  3.79 us (3%)
  local copies, waits for them, and re-layouts  2.56 us (2%)
    ppermute x21, starting transfers between devices, over_z(): return lax.ppermute(array, 'dp', [(i, (i + shift) % NZ) for i in range(NZ)])  29.7 us
    ppermute x21, waiting for transfers between devices, over_z(): return lax.ppermute(array, 'dp', [(i, (i + shift) % NZ) for i in range(NZ)])  25.8 us
    all_to_all x3, starting transfers between devices, plane_exchange(): return lax.all_to_all(array, 'mem', 0, 0, axis_index_groups=groups)  16.9 us
    all_to_all x3, waiting for transfers between devices, plane_exchange(): return lax.all_to_all(array, 'mem', 0, 0, axis_index_groups=groups)  15.6 us
    pallas_call x1, Pallas kernels, backward(): pl.pallas_call(bwd_kernel, out_shape=tuple(outs), in_specs=[smem] + [vmem...  14.5 us
    pallas_call x2, Pallas kernels, forward(): pl.pallas_call(functools.partial(fwd_kernel, groups, start), out_shape=ja...  10.4 us
    pallas_call x1, Pallas kernels, make_list(): pl.pallas_call(list_kernel, out_shape=jax.ShapeDtypeStruct((COUNT + 8,),...  4.95 us
    ppermute x3, waiting for transfers between devices, swap_cores(): return lax.ppermute(array, 'mem', [(i, i ^ 1) for i in range(2 * NCHIP)])  3.99 us
  transfers between devices with their start and end apart: 27, of which 13 were waited for; matrix products, arithmetic and copies ran while one was open for 3% of the time, Pallas kernels for 13%

profile of v3, /device:TPU:0, one launch (start us, length us, event | category | flops | bytes accessed | tf_op | source)
XLA Modules:
  0.0 137.4 jit_solution(14394993861966738218)
XLA Ops:
  0.6 4.0 %collective-permute-start.1 = (s32[16,16]{1,0:T(8,128)}, s32[16,16]{1,0:T(8,128)S(1)}, u32[]{:S(2)}, u32[]{:S(2)}) collective-permute-start(s32[16,16]{1,0:T(8,128)} %l0.1), channel_id=1, source_target_pairs={{0,64},{32,96},{64,0},{96,32},{1,65},{33,97},{65,1},{97,33},{2,66}... | collective-permute-start | bytes 3080 | tf_op jit(solution)/shard_map/ppermute | solution.py:43
  7.3 3.6 %prepare.1 = (bf16[8,128,128]{2,1,0:T(8,128)(2,1)}, bf16[8,128,128]{2,1,0:T(8,128)(2,1)}, bf16[16,256,128]{2,1,0:T(8,128)(2,1)}) custom-call(s32[3]{0:T(128)} %pad_add_fusion.place, bf16[2048,2048]{1,0:T(8,128)(2,1)} %queries.1, bf16[2048,2048]{1,0:T(8,128)(2,1)} %grads.1, bf16[512,2048]{1,0:T(8,128)(2,1)} %keys.1, bf16[512,2048]{1,0:T(8,128)(2,1)} %values.1), custom_call_target="tpu_custom_call" | custom-call | tf_op jit(solution)/shard_map/prepare/pallas_call | solution.py:79
  11.0 7.2 %all-to-all-start = ((bf16[16,256,128]{2,1,0:T(8,128)(2,1)}), bf16[16,256,128]{2,1,0:T(8,128)(2,1)S(1)}, u32[]{:S(2)}, u32[]{:S(2)}) async-start(bf16[16,256,128]{2,1,0:T(8,128)(2,1)} %get-tuple-element.30), calls=%async_computation | async-start | bytes 2097152 | tf_op jit(solution)/shard_map/all_to_all | solution.py:52
  21.3 2.2 %collective-permute-start.4 = (bf16[8,128,128]{2,1,0:T(8,128)(2,1)S(1)}, bf16[8,128,128]{2,1,0:T(8,128)(2,1)S(1)}, u32[]{:S(2)}, u32[]{:S(2)}) collective-permute-start(bf16[8,128,128]{2,1,0:T(8,128)(2,1)S(1)} %copy-done.1), channel_id=1, source_target_pairs={{0,96},{32,0},{64,32},{96,64},{1,97},{33,1},{65,33},{97,65},{2,98}... | collective-permute-start | bytes 786440 | tf_op jit(solution)/shard_map/ppermute | solution.py:43
  23.5 4.9 %entry_list.1.ents = s32[536]{0:T(1024)S(1)} custom-call(s32[3]{0:T(128)S(1)} %copy-done.2, s32[16,16]{1,0:T(8,128)S(1)} %copy-done.3, s32[16,16]{1,0:T(8,128)S(1)} %collective-permute-done.l1, s32[16,16]{1,0:T(8,128)S(1)} %collective-permute-done.1.l2, s32[16,16]{1,0:T(8,128)S(1)} %collective-permute-done.2.l3, s32[128]{0:T(128)S(1)} %copy-done.4), custom_call_target="tpu_custom_call" | custom-call | tf_op jit(solution)/shard_map/entry_list/pallas_call | solution.py:127
  30.6 3.0 %collective-permute-done.5.refs_5_.g3 = bf16[8,128,128]{2,1,0:T(8,128)(2,1)S(1)} collective-permute-done((bf16[8,128,128]{2,1,0:T(8,128)(2,1)S(1)}, bf16[8,128,128]{2,1,0:T(8,128)(2,1)S(1)}, u32[]{:S(2)}, u32[]{:S(2)}) %collective-permute-start.5) | collective-permute-done | bytes 262176 | tf_op jit(solution)/shard_map/ppermute | solution.py:43
  35.5 2.2 %collective-permute-start.9 = (bf16[8,128,128]{2,1,0:T(8,128)(2,1)S(1)}, bf16[8,128,128]{2,1,0:T(8,128)(2,1)S(1)}, u32[]{:S(2)}, u32[]{:S(2)}) collective-permute-start(bf16[8,128,128]{2,1,0:T(8,128)(2,1)S(1)} %collective-permute-done.4.refs_4_.g1), channel_id=1, source_target_pairs={{0,96},{32,0},{64,32},{96,64},{1,97},{33,1},{65,33},{97,65},{2,98}... | collective-permute-start | bytes 786440 | tf_op jit(solution)/shard_map/ppermute | solution.py:43
  37.8 7.0 %forward.2.before = f32[3,32,128]{2,1,0:T(8,128)S(1)} custom-call(s32[536]{0:T(1024)S(1)} %entry_list.1.ents, f32[3,32,128]{2,1,0:T(8,128)S(1)} %broadcast_in_dim.3.before, bf16[8,128,128]{2,1,0:T(8,128)(2,1)S(1)} %copy-done, bf16[8,128,128]{2,1,0:T(8,128)(2,1)S(1)} %collective-permute-done.6.refs_1_.q1, ...), custom_call_target="tpu_custom_call" | custom-call | tf_op jit(solution)/shard_map/forward/pallas_call | solution.py:210
  44.8 3.4 %forward.3.s0 = f32[3,32,128]{2,1,0:T(8,128)S(1)} custom-call(s32[536]{0:T(1024)S(1)} %entry_list.1.ents, f32[3,32,128]{2,1,0:T(8,128)S(1)} %forward.2.before, bf16[8,128,128]{2,1,0:T(8,128)(2,1)S(1)} %collective-permute-done.8.refs_0_.q2, bf16[8,128,128]{2,1,0:T(8,128)(2,1)S(1)} %collective-permute-done.9.refs_1_.g2, ...), custom_call_target="tpu_custom_call" | custom-call | tf_op jit(solution)/shard_map/forward/pallas_call | solution.py:210
  48.2 2.2 %collective-permute-start.12 = (f32[3,32,128]{2,1,0:T(8,128)S(1)}, f32[3,32,128]{2,1,0:T(8,128)S(1)}, u32[]{:S(2)}, u32[]{:S(2)}) collective-permute-start(f32[3,32,128]{2,1,0:T(8,128)S(1)} %forward.3.s0), channel_id=1, source_target_pairs={{0,96},{32,0},{64,32},{96,64},{1,97},{33,1},{65,33},{97,65},{2,98}... | collective-permute-start | bytes 147464 | tf_op jit(solution)/shard_map/ppermute | solution.py:43
  52.9 3.2 %collective-permute-done.11.s2 = f32[3,32,128]{2,1,0:T(8,128)S(1)} collective-permute-done((f32[3,32,128]{2,1,0:T(8,128)S(1)}, f32[3,32,128]{2,1,0:T(8,128)S(1)}, u32[]{:S(2)}, u32[]{:S(2)}) %collective-permute-start.11) | collective-permute-done | bytes 49184 | tf_op jit(solution)/shard_map/ppermute | solution.py:43
  56.2 14.5 %backward.1 = (f32[8,128,128]{2,1,0:T(8,128)S(1)}, bf16[8,128,128]{2,1,0:T(8,128)(2,1)S(1)}, bf16[8,128,128]{2,1,0:T(8,128)(2,1)S(1)}, bf16[8,128,128]{2,1,0:T(8...) custom-call(s32[536]{0:T(1024)S(1)} %entry_list.1.ents, f32[3,32,128]{2,1,0:T(8,128)S(1)} %forward.3.s0, ...), custom_call_target="tpu_custom_call" | custom-call | tf_op jit(solution)/shard_map/backward/pallas_call | solution.py:312
  72.1 2.7 %collective-permute-done.17 = bf16[16,256,128]{2,1,0:T(8,128)(2,1)S(1)} collective-permute-done((bf16[16,256,128]{2,1,0:T(8,128)(2,1)S(1)}, bf16[16,256,128]{2,1,0:T(8,128)(2,1)S(1)}, u32[]{:S(2)}, u32[]{:S(2)}) %collective-permute-start.17) | collective-permute-done | bytes 1048608 | tf_op jit(solution)/shard_map/ppermute | solution.py:47
  76.0 6.2 %all-to-all-start.1 = ((bf16[16,256,128]{2,1,0:T(8,128)(2,1)}), bf16[16,256,128]{2,1,0:T(8,128)(2,1)S(1)}, u32[]{:S(2)}, u32[]{:S(2)}) async-start(bf16[16,256,128]{2,1,0:T(8,128)(2,1)} %add_convert_fusion), calls=%async_computation.1 | async-start | bytes 2097152 | tf_op jit(solution)/shard_map/all_to_all | solution.py:52
  82.4 3.2 %collective-permute-start.14 = (bf16[8,128,128]{2,1,0:T(8,128)(2,1)S(1)}, bf16[8,128,128]{2,1,0:T(8,128)(2,1)}, u32[]{:S(2)}, u32[]{:S(2)}) collective-permute-start(bf16[8,128,128]{2,1,0:T(8,128)(2,1)S(1)} %copy-done.6), channel_id=1, source_target_pairs={{0,96},{32,0},{64,32},{96,64},{1,97},{33,1},{65,33},{97,65},{2,98}... | collective-permute-start | bytes 786440 | tf_op jit(solution)/shard_map/ppermute | solution.py:43
  85.6 14.8 %all-to-all-done.1 = bf16[16,256,128]{2,1,0:T(8,128)(2,1)S(1)} async-done(((bf16[16,256,128]{2,1,0:T(8,128)(2,1)}), bf16[16,256,128]{2,1,0:T(8,128)(2,1)S(1)}, u32[]{:S(2)}, u32[]{:S(2)}) %all-to-all-start.1) | async-done | bytes 1048608 | tf_op jit(solution)/shard_map/all_to_all | solution.py:52
  100.8 3.2 %collective-permute-start.19 = (bf16[128,2048]{1,0:T(8,128)(2,1)S(1)}, bf16[128,2048]{1,0:T(8,128)(2,1)S(1)}, u32[]{:S(2)}, u32[]{:S(2)}) collective-permute-start(bf16[128,2048]{1,0:T(8,128)(2,1)S(1)} %bitcast.21), channel_id=1, source_target_pairs={{0,96},{32,0},{64,32},{96,64},{1,97},{33,1},{65,33},{97,65},{2,98}... | collective-permute-start | bytes 1572872 | tf_op jit(solution)/shard_map/ppermute | solution.py:43
  109.6 7.3 %collective-permute-done.18.v3 = bf16[128,2048]{1,0:T(8,128)(2,1)S(1)} collective-permute-done((bf16[128,2048]{1,0:T(8,128)(2,1)S(1)}, bf16[128,2048]{1,0:T(8,128)(2,1)S(1)}, u32[]{:S(2)}, u32[]{:S(2)}) %collective-permute-start.18) | collective-permute-done | bytes 524320 | tf_op jit(solution)/shard_map/ppermute | solution.py:43
  116.9 3.5 %all-to-all-start.2 = ((bf16[16,64,128]{2,1,0:T(8,128)(2,1)}), bf16[16,64,128]{2,1,0:T(8,128)(2,1)S(1)}, u32[]{:S(2)}, u32[]{:S(2)}) async-start(bf16[16,64,128]{2,1,0:T(8,128)(2,1)} %maximum_select_fusion), calls=%async_computation.2 | async-start | bytes 524288 | tf_op jit(solution)/shard_map/all_to_all | solution.py:52
  120.5 3.3 %collective-permute-start.20 = (bf16[128,2048]{1,0:T(8,128)(2,1)S(1)}, bf16[128,2048]{1,0:T(8,128)(2,1)}, u32[]{:S(2)}, u32[]{:S(2)}) collective-permute-start(bf16[128,2048]{1,0:T(8,128)(2,1)S(1)} %collective-permute-done.19.k1), channel_id=1, source_target_pairs={{0,96},{32,0},{64,32},{96,64},{1,97},{33,1},{65,33},{97,65},{2,98}... | collective-permute-start | bytes 1572872 | tf_op jit(solution)/shard_map/ppermute | solution.py:43
  123.8 3.9 %collective-permute-done.23.v1 = bf16[128,2048]{1,0:T(8,128)(2,1)S(1)} collective-permute-done((bf16[128,2048]{1,0:T(8,128)(2,1)S(1)}, bf16[128,2048]{1,0:T(8,128)(2,1)S(1)}, u32[]{:S(2)}, u32[]{:S(2)}) %collective-permute-start.23) | collective-permute-done | bytes 524320 | tf_op jit(solution)/shard_map/ppermute | solution.py:43
  127.7 2.3 %place_near.1 = (bf16[512,2048]{1,0:T(8,128)(2,1)}, bf16[512,2048]{1,0:T(8,128)(2,1)}) custom-call(s32[3]{0:T(128)S(1)} %copy-done.2, bf16[128,2048]{1,0:T(8,128)(2,1)S(1)} %bitcast.23, bf16[128,2048]{1,0:T(8,128)(2,1)S(1)} %collective-permute-done.19.k1, bf16[128,2048]{1,0:T(8,128)(2,1)S(1)} %collective-permute-done.22.k3, bf16[128,2048]{1,0:T(8,128)(2,1)S(1)} %bitcast.26, ...), custom_call_target="tpu_custom_call" | custom-call | tf_op jit(solution)/shard_map/place_near/pallas_call | solution.py:359
  130.7 3.7 %collective-permute-done.20.k2 = bf16[128,2048]{1,0:T(8,128)(2,1)} collective-permute-done((bf16[128,2048]{1,0:T(8,128)(2,1)S(1)}, bf16[128,2048]{1,0:T(8,128)(2,1)}, u32[]{:S(2)}, u32[]{:S(2)}) %collective-permute-start.20) | collective-permute-done | bytes 524320 | tf_op jit(solution)/shard_map/ppermute | solution.py:43
  135.2 2.2 %place_far.1 = (bf16[512,2048]{1,0:T(8,128)(2,1)}, bf16[512,2048]{1,0:T(8,128)(2,1)}) custom-call(s32[3]{0:T(128)S(1)} %copy-done.2, bf16[128,2048]{1,0:T(8,128)(2,1)} %collective-permute-done.20.k2, bf16[128,2048]{1,0:T(8,128)(2,1)} %collective-permute-done.21.v2, ...), custom_call_target="tpu_custom_call", output_to_operand_aliasing={{0}: (3, {}), {1}: (4, {})} | custom-call | tf_op jit(solution)/shard_map/place_far/pallas_call | solution.py:375
  (65 shorter events, 22.7 us)
Async XLA Ops:
  0.6 10.3 %collective-permute-start.1 = (s32[16,16]{1,0:T(8,128)}, s32[16,16]{1,0:T(8,128)S(1)}, u32[]{:S(2)}, u32[]{:S(2)}) collective-permute-start(s32[16,16]{1,0:T(8,128)} %l0.1), channel_id=1, source_target_pairs={{0,64},{32,96},{64,0},{96,32},{1,65},{33,97},{65,1},{97,33},{2,66}... | collective-permute-start | bytes 3080 | tf_op jit(solution)/shard_map/ppermute | solution.py:43
  4.7 6.3 %collective-permute-start = (s32[16,16]{1,0:T(8,128)}, s32[16,16]{1,0:T(8,128)S(1)}, u32[]{:S(2)}, u32[]{:S(2)}) collective-permute-start(s32[16,16]{1,0:T(8,128)} %l0.1), channel_id=1, source_target_pairs={{0,96},{32,0},{64,32},{96,64},{1,97},{33,1},{65,33},{97,65},{2,98}... | collective-permute-start | bytes 3080 | tf_op jit(solution)/shard_map/ppermute | solution.py:43
  5.4 5.6 %collective-permute-start.2 = (s32[16,16]{1,0:T(8,128)}, s32[16,16]{1,0:T(8,128)S(1)}, u32[]{:S(2)}, u32[]{:S(2)}) collective-permute-start(s32[16,16]{1,0:T(8,128)} %l0.1), channel_id=1, source_target_pairs={{0,32},{32,64},{64,96},{96,0},{1,33},{33,65},{65,97},{97,1},{2,34}... | collective-permute-start | bytes 3080 | tf_op jit(solution)/shard_map/ppermute | solution.py:43
  11.0 23.5 %all-to-all-start = ((bf16[16,256,128]{2,1,0:T(8,128)(2,1)}), bf16[16,256,128]{2,1,0:T(8,128)(2,1)S(1)}, u32[]{:S(2)}, u32[]{:S(2)}) async-start(bf16[16,256,128]{2,1,0:T(8,128)(2,1)} %get-tuple-element.30), calls=%async_computation | async-start | bytes 2097152 | tf_op jit(solution)/shard_map/all_to_all | solution.py:52
  18.2 10.3 %collective-permute-start.6 = (bf16[8,128,128]{2,1,0:T(8,128)(2,1)S(1)}, bf16[8,128,128]{2,1,0:T(8,128)(2,1)S(1)}, u32[]{:S(2)}, u32[]{:S(2)}) collective-permute-start(bf16[8,128,128]{2,1,0:T(8,128)(2,1)S(1)} %copy-done), channel_id=1, source_target_pairs={{0,96},{32,0},{64,32},{96,64},{1,97},{33,1},{65,33},{97,65},{2,98}... | collective-permute-start | bytes 786440 | tf_op jit(solution)/shard_map/ppermute | solution.py:43
  20.2 10.5 %collective-permute-start.3 = (bf16[8,128,128]{2,1,0:T(8,128)(2,1)S(1)}, bf16[8,128,128]{2,1,0:T(8,128)(2,1)S(1)}, u32[]{:S(2)}, u32[]{:S(2)}) collective-permute-start(bf16[8,128,128]{2,1,0:T(8,128)(2,1)S(1)} %copy-done), channel_id=1, source_target_pairs={{0,32},{32,64},{64,96},{96,0},{1,33},{33,65},{65,97},{97,1},{2,34}... | collective-permute-start | bytes 786440 | tf_op jit(solution)/shard_map/ppermute | solution.py:43
  20.3 13.4 %collective-permute-start.5 = (bf16[8,128,128]{2,1,0:T(8,128)(2,1)S(1)}, bf16[8,128,128]{2,1,0:T(8,128)(2,1)S(1)}, u32[]{:S(2)}, u32[]{:S(2)}) collective-permute-start(bf16[8,128,128]{2,1,0:T(8,128)(2,1)S(1)} %copy-done.1), channel_id=1, source_target_pairs={{0,32},{32,64},{64,96},{96,0},{1,33},{33,65},{65,97},{97,1},{2,34}... | collective-permute-start | bytes 786440 | tf_op jit(solution)/shard_map/ppermute | solution.py:43
  21.3 12.4 %collective-permute-start.4 = (bf16[8,128,128]{2,1,0:T(8,128)(2,1)S(1)}, bf16[8,128,128]{2,1,0:T(8,128)(2,1)S(1)}, u32[]{:S(2)}, u32[]{:S(2)}) collective-permute-start(bf16[8,128,128]{2,1,0:T(8,128)(2,1)S(1)} %copy-done.1), channel_id=1, source_target_pairs={{0,96},{32,0},{64,32},{96,64},{1,97},{33,1},{65,33},{97,65},{2,98}... | collective-permute-start | bytes 786440 | tf_op jit(solution)/shard_map/ppermute | solution.py:43
  34.5 10.3 %collective-permute-start.8 = (bf16[8,128,128]{2,1,0:T(8,128)(2,1)S(1)}, bf16[8,128,128]{2,1,0:T(8,128)(2,1)S(1)}, u32[]{:S(2)}, u32[]{:S(2)}) collective-permute-start(bf16[8,128,128]{2,1,0:T(8,128)(2,1)S(1)} %collective-permute-done.3.refs_2_.q3), channel_id=1, source_target_pairs={{0,32},{32,64},{64,96},{96,0},{1,33},{33,65},{65,97},{97,1},{2,34}... | collective-permute-start | bytes 786440 | tf_op jit(solution)/shard_map/ppermute | solution.py:43
  35.5 9.3 %collective-permute-start.9 = (bf16[8,128,128]{2,1,0:T(8,128)(2,1)S(1)}, bf16[8,128,128]{2,1,0:T(8,128)(2,1)S(1)}, u32[]{:S(2)}, u32[]{:S(2)}) collective-permute-start(bf16[8,128,128]{2,1,0:T(8,128)(2,1)S(1)} %collective-permute-done.4.refs_4_.g1), channel_id=1, source_target_pairs={{0,96},{32,0},{64,32},{96,64},{1,97},{33,1},{65,33},{97,65},{2,98}... | collective-permute-start | bytes 786440 | tf_op jit(solution)/shard_map/ppermute | solution.py:43
  48.2 4.6 %collective-permute-start.12 = (f32[3,32,128]{2,1,0:T(8,128)S(1)}, f32[3,32,128]{2,1,0:T(8,128)S(1)}, u32[]{:S(2)}, u32[]{:S(2)}) collective-permute-start(f32[3,32,128]{2,1,0:T(8,128)S(1)} %forward.3.s0), channel_id=1, source_target_pairs={{0,96},{32,0},{64,32},{96,64},{1,97},{33,1},{65,33},{97,65},{2,98}... | collective-permute-start | bytes 147464 | tf_op jit(solution)/shard_map/ppermute | solution.py:43
  50.4 5.6 %collective-permute-start.11 = (f32[3,32,128]{2,1,0:T(8,128)S(1)}, f32[3,32,128]{2,1,0:T(8,128)S(1)}, u32[]{:S(2)}, u32[]{:S(2)}) collective-permute-start(f32[3,32,128]{2,1,0:T(8,128)S(1)} %forward.3.s0), channel_id=1, source_target_pairs={{0,64},{32,96},{64,0},{96,32},{1,65},{33,97},{65,1},{97,33},{2,66}... | collective-permute-start | bytes 147464 | tf_op jit(solution)/shard_map/ppermute | solution.py:43
  50.4 5.8 %collective-permute-start.10 = (f32[3,32,128]{2,1,0:T(8,128)S(1)}, f32[3,32,128]{2,1,0:T(8,128)S(1)}, u32[]{:S(2)}, u32[]{:S(2)}) collective-permute-start(f32[3,32,128]{2,1,0:T(8,128)S(1)} %forward.3.s0), channel_id=1, source_target_pairs={{0,32},{32,64},{64,96},{96,0},{1,33},{33,65},{65,97},{97,1},{2,34}... | collective-permute-start | bytes 147464 | tf_op jit(solution)/shard_map/ppermute | solution.py:43
  76.0 24.3 %all-to-all-start.1 = ((bf16[16,256,128]{2,1,0:T(8,128)(2,1)}), bf16[16,256,128]{2,1,0:T(8,128)(2,1)S(1)}, u32[]{:S(2)}, u32[]{:S(2)}) async-start(bf16[16,256,128]{2,1,0:T(8,128)(2,1)} %add_convert_fusion), calls=%async_computation.1 | async-start | bytes 2097152 | tf_op jit(solution)/shard_map/all_to_all | solution.py:52
  82.3 21.8 %collective-permute-start.13 = (bf16[8,128,128]{2,1,0:T(8,128)(2,1)S(1)}, bf16[8,128,128]{2,1,0:T(8,128)(2,1)}, u32[]{:S(2)}, u32[]{:S(2)}) collective-permute-start(bf16[8,128,128]{2,1,0:T(8,128)(2,1)S(1)} %copy-done.8), channel_id=1, source_target_pairs={{0,32},{32,64},{64,96},{96,0},{1,33},{33,65},{65,97},{97,1},{2,34}... | collective-permute-start | bytes 786440 | tf_op jit(solution)/shard_map/ppermute | solution.py:43
  82.4 21.7 %collective-permute-start.14 = (bf16[8,128,128]{2,1,0:T(8,128)(2,1)S(1)}, bf16[8,128,128]{2,1,0:T(8,128)(2,1)}, u32[]{:S(2)}, u32[]{:S(2)}) collective-permute-start(bf16[8,128,128]{2,1,0:T(8,128)(2,1)S(1)} %copy-done.6), channel_id=1, source_target_pairs={{0,96},{32,0},{64,32},{96,64},{1,97},{33,1},{65,33},{97,65},{2,98}... | collective-permute-start | bytes 786440 | tf_op jit(solution)/shard_map/ppermute | solution.py:43
  85.6 18.5 %collective-permute-start.15 = (bf16[8,128,128]{2,1,0:T(8,128)(2,1)S(1)}, bf16[8,128,128]{2,1,0:T(8,128)(2,1)}, u32[]{:S(2)}, u32[]{:S(2)}) collective-permute-start(bf16[8,128,128]{2,1,0:T(8,128)(2,1)S(1)} %get-tuple-element.45), channel_id=1, source_target_pairs={{0,64},{32,96},{64,0},{96,32},{1,65},{33,97},{65,1},{97,33},{2,66}... | collective-permute-start | bytes 786440 | tf_op jit(solution)/shard_map/ppermute | solution.py:43
  100.8 16.1 %collective-permute-start.18 = (bf16[128,2048]{1,0:T(8,128)(2,1)S(1)}, bf16[128,2048]{1,0:T(8,128)(2,1)S(1)}, u32[]{:S(2)}, u32[]{:S(2)}) collective-permute-start(bf16[128,2048]{1,0:T(8,128)(2,1)S(1)} %bitcast.24), channel_id=1, source_target_pairs={{0,32},{32,64},{64,96},{96,0},{1,33},{33,65},{65,97},{97,1},{2,34}... | collective-permute-start | bytes 1572872 | tf_op jit(solution)/shard_map/ppermute | solution.py:43
  100.8 16.1 %collective-permute-start.19 = (bf16[128,2048]{1,0:T(8,128)(2,1)S(1)}, bf16[128,2048]{1,0:T(8,128)(2,1)S(1)}, u32[]{:S(2)}, u32[]{:S(2)}) collective-permute-start(bf16[128,2048]{1,0:T(8,128)(2,1)S(1)} %bitcast.21), channel_id=1, source_target_pairs={{0,96},{32,0},{64,32},{96,64},{1,97},{33,1},{65,33},{97,65},{2,98}... | collective-permute-start | bytes 1572872 | tf_op jit(solution)/shard_map/ppermute | solution.py:43
  105.3 22.4 %collective-permute-start.23 = (bf16[128,2048]{1,0:T(8,128)(2,1)S(1)}, bf16[128,2048]{1,0:T(8,128)(2,1)S(1)}, u32[]{:S(2)}, u32[]{:S(2)}) collective-permute-start(bf16[128,2048]{1,0:T(8,128)(2,1)S(1)} %bitcast.25), channel_id=1, source_target_pairs={{0,96},{32,0},{64,32},{96,64},{1,97},{33,1},{65,33},{97,65},{2,98}... | collective-permute-start | bytes 1572872 | tf_op jit(solution)/shard_map/ppermute | solution.py:43
  105.4 22.3 %collective-permute-start.22 = (bf16[128,2048]{1,0:T(8,128)(2,1)S(1)}, bf16[128,2048]{1,0:T(8,128)(2,1)S(1)}, u32[]{:S(2)}, u32[]{:S(2)}) collective-permute-start(bf16[128,2048]{1,0:T(8,128)(2,1)S(1)} %bitcast.22), channel_id=1, source_target_pairs={{0,32},{32,64},{64,96},{96,0},{1,33},{33,65},{65,97},{97,1},{2,34}... | collective-permute-start | bytes 1572872 | tf_op jit(solution)/shard_map/ppermute | solution.py:43
  116.9 13.0 %all-to-all-start.2 = ((bf16[16,64,128]{2,1,0:T(8,128)(2,1)}), bf16[16,64,128]{2,1,0:T(8,128)(2,1)S(1)}, u32[]{:S(2)}, u32[]{:S(2)}) async-start(bf16[16,64,128]{2,1,0:T(8,128)(2,1)} %maximum_select_fusion), calls=%async_computation.2 | async-start | bytes 524288 | tf_op jit(solution)/shard_map/all_to_all | solution.py:52
  120.5 13.9 %collective-permute-start.20 = (bf16[128,2048]{1,0:T(8,128)(2,1)S(1)}, bf16[128,2048]{1,0:T(8,128)(2,1)}, u32[]{:S(2)}, u32[]{:S(2)}) collective-permute-start(bf16[128,2048]{1,0:T(8,128)(2,1)S(1)} %collective-permute-done.19.k1), channel_id=1, source_target_pairs={{0,96},{32,0},{64,32},{96,64},{1,97},{33,1},{65,33},{97,65},{2,98}... | collective-permute-start | bytes 1572872 | tf_op jit(solution)/shard_map/ppermute | solution.py:43
  123.8 11.4 %collective-permute-start.21 = (bf16[128,2048]{1,0:T(8,128)(2,1)S(1)}, bf16[128,2048]{1,0:T(8,128)(2,1)}, u32[]{:S(2)}, u32[]{:S(2)}) collective-permute-start(bf16[128,2048]{1,0:T(8,128)(2,1)S(1)} %collective-permute-done.18.v3), channel_id=1, source_target_pairs={{0,32},{32,64},{64,96},{96,0},{1,33},{33,65},{65,97},{97,1},{2,34}... | collective-permute-start | bytes 1572872 | tf_op jit(solution)/shard_map/ppermute | solution.py:43
  (12 other events, 75.8 us)
